TPU v7x, 32 devices: a whole 2x2x4 slice. The times are simulated.
32 devices in a mesh: blk: 4 (over y, x), head: 8 (over z, core).
Axes of the slice: x: 2, y: 2, z: 4, core: 2. Of those that a mesh axis runs over, the one named last changes fastest.
Arguments:
- qkv: bfloat16 [16384, 6144], P(('blk', 'head')), may hold values from -12 to 12
Outputs:
- attended: bfloat16 [16384, 2048], P(('blk', 'head'))
All inputs are finite; a program needn't handle non-finite values.
Results may differ from a plain program's by a relative error of at most 0.0059.
Values may be sent and summed in bfloat16 or wider, within the bound.
No kernel may reach another device: no remote copies, remote signals or barrier semaphores. Data moves between devices by JAX's collectives and lax.ppermute only.
A program may use at most 128 MiB of HBM per device.

v0:
```python
import jax
import jax.numpy as jnp
from jax import lax
from jax.sharding import PartitionSpec as P

HEAD_DIM = 64
BLOCK = 2048
BLK_DEV = 2


def attend(query, pair):
    keys = pair[:, 0]
    values = pair[:, 1]
    tile = min(512, BLOCK)
    scale = HEAD_DIM ** (-0.5)

    def one_tile(query_tile):
        scores = (
            jnp.einsum("qhd,khd->hqk", query_tile, keys, preferred_element_type=jnp.float32) * scale
        )
        row_max = jnp.max(scores, axis=-1)
        probs = jnp.exp(scores - row_max[..., None]).astype(jnp.bfloat16)
        total = jnp.sum(probs.astype(jnp.float32), axis=-1)
        weighted = jnp.einsum("hqk,khd->hqd", probs, values, preferred_element_type=jnp.float32)
        return (row_max, total, weighted)

    tiles = query.reshape(BLOCK // tile, tile, query.shape[1], query.shape[2])
    return lax.map(one_tile, tiles)


def combine(partials):
    overall = partials[0][0]
    for entry in partials[1:]:
        overall = jnp.maximum(overall, entry[0])
    numer = jnp.zeros_like(partials[0][2])
    denom = jnp.zeros_like(partials[0][1])
    for row_max, total, weighted in partials:
        factor = jnp.exp(row_max - overall)
        numer = numer + factor[..., None] * weighted
        denom = denom + factor * total
    result = numer / denom[..., None]
    return result.transpose(0, 2, 1, 3).reshape(BLOCK, result.shape[1] * result.shape[3])


def on_device(qkv):
    rows = qkv.shape[0]
    heads_cols = qkv.shape[1] // 3
    shaped = qkv.reshape(rows, 3, heads_cols)
    grouped = lax.all_to_all(shaped, "head", split_axis=2, concat_axis=0, tiled=True)
    local_cols = grouped.shape[2]
    heads_here = local_cols // HEAD_DIM
    grid = grouped.reshape(BLK_DEV, BLOCK, 3, heads_here, HEAD_DIM)
    queries = grid[:, :, 0]
    pairs = grid[:, :, 1:3]
    device_bits = lax.axis_size("blk").bit_length() - 1
    partials = [[] for j in range(BLK_DEV)]

    def own_blocks():
        for j in range(BLK_DEV):
            partials[j].append(attend(queries[j], pairs[j]))
            partials[j].append(attend(queries[j], pairs[j ^ 1 << 0]))

    gathered = lax.all_gather(pairs, "blk", axis=0, tiled=True)
    mine = lax.axis_index("blk")
    for bit in range(device_bits):
        for j in range(BLK_DEV):
            where = jnp.bitwise_xor(mine, 1 << bit) * BLK_DEV + j
            chosen = lax.dynamic_index_in_dim(gathered, where, 0, keepdims=False)
            partials[j].append(attend(queries[j], chosen))
    own_blocks()
    outputs = jnp.concatenate([combine(partials[j]) for j in range(BLK_DEV)], axis=0).astype(
        jnp.bfloat16
    )
    return lax.all_to_all(outputs, "head", split_axis=0, concat_axis=1, tiled=True)


def solution(mesh):
    in_specs = (P(("blk", "head"), None),)
    out_specs = P(("blk", "head"), None)
    return jax.shard_map(
        on_device, mesh=mesh, in_specs=in_specs, out_specs=out_specs, check_vma=False
    )
```

profile of v0, /device:TPU:1, one launch (start us, length us, event | category | flops | bytes accessed | tf_op | source)
XLA Modules:
  0.0 946.5 jit_solution(1397758629578891517)
XLA Ops:
  6.5 8.6 copy.34
  15.1 10.5 %copy.35 = bf16[512,3,2048]{0,1,2:T(4,128)(2,1)} copy(bf16[512,3,2048]{0,2,1:T(8,128)(2,1)} %bitcast.298) | data formatting | bytes 12582912 | tf_op jit(solution)/shard_map/reshape | solution.py:48
  32.0 183.1 %all-to-all-done = bf16[512,3,2048]{0,1,2:T(4,128)(2,1)} async-done(((bf16[512,3,2048]{0,1,2:T(4,128)(2,1)}), bf16[512,3,2048]{0,1,2:T(4,128)(2,1)}, u32[]{:S(2)}, u32[]{:S(2)}) %all-to-all-start) | async-done | bytes 6291488 | tf_op jit(solution)/shard_map/all_to_all | solution.py:49
  226.3 10.4 %reshape.43 = bf16[2,2048,3,4,64]{1,0,4,3,2:T(2,128)(2,1)} reshape(bf16[8,512,3,256]{1,0,3,2:T(8,128)(2,1)} %copy.37) | data formatting | bytes 12582912 | tf_op jit(solution)/shard_map/reshape | solution.py:52
  239.5 9.9 %slice_reduce_fusion.1 = (bf16[2048,4,64]{0,2,1:T(8,128)(2,1)}, bf16[2048,4,64]{0,2,1:T(8,128)(2,1)}) fusion(bf16[2,2048,3,4,64]{1,0,4,3,2:T(2,128)(2,1)S(1)} %copy-done.12), kind=kLoop, calls=%fused_computation.97 | loop fusion | bytes 4194304 | tf_op jit(solution)/shard_map/slice | solution.py:69
  249.4 7.0 fusion.50
  260.5 7.4 copy_bitcast_fusion
  269.8 69.9 %while.114 = (s32[]{:T(128)}, f32[4,4,512]{2,1,0:T(4,128)S(1)}, f32[4,4,512]{2,1,0:T(4,128)S(1)}, f32[4,4,512,64]{2,3,1,0:T(8,128)}, bf16[4,512,4,64]{1,3,2,0:T(...) while((s32[]{:T(128)}, f32[4,4,512]{2,1,0:T(4,128)S(1)}, ...), condition=%wide.region_11.12_spmd, body=%wide.region_8.11_spmd.sunk | while | flops 1115680768 | bytes 120390264 | solution.py:28
  279.6 8.2 fusion.99
  296.0 8.2 fusion.99
  312.4 8.2 fusion.99
  331.5 8.2 fusion.99
  345.8 70.9 %while.115 = (s32[]{:T(128)}, f32[4,4,512]{2,1,0:T(4,128)S(1)}, f32[4,4,512]{2,1,0:T(4,128)S(1)}, f32[4,4,512,64]{2,3,1,0:T(8,128)}, bf16[4,512,4,64]{1,3,2,0:T(...) while((s32[]{:T(128)}, f32[4,4,512]{2,1,0:T(4,128)S(1)}, ...), condition=%wide.region_15.16_spmd, body=%wide.region_12.15_spmd.sunk | while | flops 1115680768 | bytes 120390768 | solution.py:28
  355.3 8.2 fusion.102
  373.1 8.2 fusion.102
  390.8 8.2 fusion.102
  408.5 8.2 fusion.102
  420.6 71.1 %while.118 = (s32[]{:T(128)}, f32[4,4,512]{2,1,0:T(4,128)S(1)}, f32[4,4,512]{2,1,0:T(4,128)S(1)}, f32[4,4,512,64]{2,3,1,0:T(8,128)}, bf16[4,512,4,64]{1,3,2,0:T(...) while((s32[]{:T(128)}, f32[4,4,512]{2,1,0:T(4,128)S(1)}, ...), condition=%wide.region_27.28_spmd, body=%wide.region_24.27_spmd.sunk | while | flops 1115680768 | bytes 120390768 | solution.py:28
  430.4 8.2 fusion.111
  448.1 8.2 fusion.111
  465.9 8.2 fusion.111
  483.6 8.2 fusion.111
  493.4 69.4 %while.119 = (s32[]{:T(128)}, f32[4,4,512]{2,1,0:T(4,128)S(1)}, f32[4,4,512]{2,1,0:T(4,128)S(1)}, f32[4,4,512,64]{2,3,1,0:T(8,128)}, bf16[4,512,4,64]{1,3,2,0:T(...) while((s32[]{:T(128)}, f32[4,4,512]{2,1,0:T(4,128)S(1)}, ...), condition=%wide.region_31.32_spmd, body=%wide.region_28.31_spmd.sunk | while | flops 1115680768 | bytes 120390768 | solution.py:28
  502.6 8.2 fusion.114
  519.9 8.2 fusion.114
  537.2 8.2 fusion.114
  554.6 8.2 fusion.114
  572.8 77.1 %while.112 = (s32[]{:T(128)}, f32[4,4,512]{2,1,0:T(4,128)S(1)}, f32[4,4,512]{2,1,0:T(4,128)S(1)}, f32[4,4,512,64]{2,3,1,0:T(8,128)}, bf16[4,512,4,64]{1,3,2,0:T(...) while((s32[]{:T(128)}, f32[4,4,512]{2,1,0:T(4,128)S(1)}, ...), condition=%wide.region_3.4_spmd, body=%wide.region_0.3_spmd.sunk | while | flops 1115680768 | bytes 120390264 | solution.py:28
  582.4 9.8 %fusion.93 = f32[4,4,512,64]{2,3,1,0:T(8,128)} fusion(f32[4,4,512,64]{2,3,1,0:T(8,128)} %get-tuple-element.1314, s32[]{:T(128)} %get-tuple-element.1311, bf16[2048,4,64]{0,2,1:T(8,128)(2,1)} %get-tuple-element.1325, f32[4,512,2048]{2,1,0:T(8,128)} %copy-done.4, f32[4,512]{1,0:T(4,128)S(1)} %get-tuple-element.1054), kind=kOutput, calls=%fused_computation.4.clone.1 | convolution fusion | flops 549453824 | bytes 18358784 | tf_op jit(solution)/shard_map/while/body/eval_jaxpr/hqk,khd->hqd/dot_general | solution.py:24
  601.6 9.8 %fusion.93 = f32[4,4,512,64]{2,3,1,0:T(8,128)} fusion(f32[4,4,512,64]{2,3,1,0:T(8,128)} %get-tuple-element.1314, s32[]{:T(128)} %get-tuple-element.1311, bf16[2048,4,64]{0,2,1:T(8,128)(2,1)} %get-tuple-element.1325, f32[4,512,2048]{2,1,0:T(8,128)} %copy-done.4, f32[4,512]{1,0:T(4,128)S(1)} %get-tuple-element.1054), kind=kOutput, calls=%fused_computation.4.clone.1 | convolution fusion | flops 549453824 | bytes 18358784 | tf_op jit(solution)/shard_map/while/body/eval_jaxpr/hqk,khd->hqd/dot_general | solution.py:24
  620.8 9.8 %fusion.93 = f32[4,4,512,64]{2,3,1,0:T(8,128)} fusion(f32[4,4,512,64]{2,3,1,0:T(8,128)} %get-tuple-element.1314, s32[]{:T(128)} %get-tuple-element.1311, bf16[2048,4,64]{0,2,1:T(8,128)(2,1)} %get-tuple-element.1325, f32[4,512,2048]{2,1,0:T(8,128)} %copy-done.4, f32[4,512]{1,0:T(4,128)S(1)} %get-tuple-element.1054), kind=kOutput, calls=%fused_computation.4.clone.1 | convolution fusion | flops 549453824 | bytes 18358784 | tf_op jit(solution)/shard_map/while/body/eval_jaxpr/hqk,khd->hqd/dot_general | solution.py:24
  640.1 9.8 %fusion.93 = f32[4,4,512,64]{2,3,1,0:T(8,128)} fusion(f32[4,4,512,64]{2,3,1,0:T(8,128)} %get-tuple-element.1314, s32[]{:T(128)} %get-tuple-element.1311, bf16[2048,4,64]{0,2,1:T(8,128)(2,1)} %get-tuple-element.1325, f32[4,512,2048]{2,1,0:T(8,128)} %copy-done.4, f32[4,512]{1,0:T(4,128)S(1)} %get-tuple-element.1054), kind=kOutput, calls=%fused_computation.4.clone.1 | convolution fusion | flops 549453824 | bytes 18358784 | tf_op jit(solution)/shard_map/while/body/eval_jaxpr/hqk,khd->hqd/dot_general | solution.py:24
  651.6 66.0 %while.113 = (s32[]{:T(128)}, f32[4,4,512]{2,1,0:T(4,128)S(1)}, f32[4,4,512]{2,1,0:T(4,128)S(1)}, f32[4,4,512,64]{2,3,1,0:T(8,128)}, bf16[4,512,4,64]{1,3,2,0:T(...) while((s32[]{:T(128)}, f32[4,4,512]{2,1,0:T(4,128)S(1)}, ...), condition=%wide.region_7.8_spmd, body=%wide.region_4.7_spmd.sunk | while | flops 1115680768 | bytes 120390264 | solution.py:28
  659.8 8.2 fusion.96
  676.2 8.2 fusion.96
  692.6 8.2 fusion.96
  708.9 8.2 fusion.96
  728.0 76.9 %while.116 = (s32[]{:T(128)}, f32[4,4,512]{2,1,0:T(4,128)S(1)}, f32[4,4,512]{2,1,0:T(4,128)S(1)}, f32[4,4,512,64]{2,3,1,0:T(8,128)}, bf16[4,512,4,64]{1,3,2,0:T(...) while((s32[]{:T(128)}, f32[4,4,512]{2,1,0:T(4,128)S(1)}, ...), condition=%wide.region_19.20_spmd, body=%wide.region_16.19_spmd.sunk | while | flops 1115680768 | bytes 120390264 | solution.py:28
  737.4 9.8 %fusion.105 = f32[4,4,512,64]{2,3,1,0:T(8,128)} fusion(f32[4,4,512,64]{2,3,1,0:T(8,128)} %get-tuple-element.1218, s32[]{:T(128)} %get-tuple-element.1215, bf16[2048,4,64]{0,2,1:T(8,128)(2,1)} %get-tuple-element.1229, f32[4,512,2048]{2,1,0:T(8,128)} %copy-done.6, f32[4,512]{1,0:T(4,128)S(1)} %get-tuple-element.1098), kind=kOutput, calls=%fused_computation.52.clone.1 | convolution fusion | flops 549453824 | bytes 18358784 | tf_op jit(solution)/shard_map/while/body/eval_jaxpr/hqk,khd->hqd/dot_general | solution.py:24
  756.6 9.8 %fusion.105 = f32[4,4,512,64]{2,3,1,0:T(8,128)} fusion(f32[4,4,512,64]{2,3,1,0:T(8,128)} %get-tuple-element.1218, s32[]{:T(128)} %get-tuple-element.1215, bf16[2048,4,64]{0,2,1:T(8,128)(2,1)} %get-tuple-element.1229, f32[4,512,2048]{2,1,0:T(8,128)} %copy-done.6, f32[4,512]{1,0:T(4,128)S(1)} %get-tuple-element.1098), kind=kOutput, calls=%fused_computation.52.clone.1 | convolution fusion | flops 549453824 | bytes 18358784 | tf_op jit(solution)/shard_map/while/body/eval_jaxpr/hqk,khd->hqd/dot_general | solution.py:24
  775.8 9.8 %fusion.105 = f32[4,4,512,64]{2,3,1,0:T(8,128)} fusion(f32[4,4,512,64]{2,3,1,0:T(8,128)} %get-tuple-element.1218, s32[]{:T(128)} %get-tuple-element.1215, bf16[2048,4,64]{0,2,1:T(8,128)(2,1)} %get-tuple-element.1229, f32[4,512,2048]{2,1,0:T(8,128)} %copy-done.6, f32[4,512]{1,0:T(4,128)S(1)} %get-tuple-element.1098), kind=kOutput, calls=%fused_computation.52.clone.1 | convolution fusion | flops 549453824 | bytes 18358784 | tf_op jit(solution)/shard_map/while/body/eval_jaxpr/hqk,khd->hqd/dot_general | solution.py:24
  795.1 9.8 %fusion.105 = f32[4,4,512,64]{2,3,1,0:T(8,128)} fusion(f32[4,4,512,64]{2,3,1,0:T(8,128)} %get-tuple-element.1218, s32[]{:T(128)} %get-tuple-element.1215, bf16[2048,4,64]{0,2,1:T(8,128)(2,1)} %get-tuple-element.1229, f32[4,512,2048]{2,1,0:T(8,128)} %copy-done.6, f32[4,512]{1,0:T(4,128)S(1)} %get-tuple-element.1098), kind=kOutput, calls=%fused_computation.52.clone.1 | convolution fusion | flops 549453824 | bytes 18358784 | tf_op jit(solution)/shard_map/while/body/eval_jaxpr/hqk,khd->hqd/dot_general | solution.py:24
  806.5 65.7 %while.117 = (s32[]{:T(128)}, f32[4,4,512]{2,1,0:T(4,128)S(1)}, f32[4,4,512]{2,1,0:T(4,128)S(1)}, f32[4,4,512,64]{2,3,1,0:T(8,128)}, bf16[4,512,4,64]{1,3,2,0:T(...) while((s32[]{:T(128)}, f32[4,4,512]{2,1,0:T(4,128)S(1)}, ...), condition=%wide.region_23.24_spmd, body=%wide.region_20.23_spmd.sunk | while | flops 1115680768 | bytes 120390264 | solution.py:28
  814.9 8.2 fusion.108
  831.3 8.2 fusion.108
  847.6 8.2 fusion.108
  864.0 8.2 fusion.108
  880.9 52.2 %all_to_all.31 = bf16[8,512,256]{2,1,0:T(8,128)(2,1)S(1)} all-to-all(bf16[8,512,256]{2,1,0:T(8,128)(2,1)} %bitcast.299), channel_id=1, replica_groups=mesh['blk'=4,'head'=8] {'head'}, dimensions={0} | all-to-all | bytes 4194304 | tf_op jit(solution)/shard_map/all_to_all | solution.py:74
  (268 shorter events, 366.5 us)
Async XLA Ops:
  25.6 189.5 %all-to-all-start = ((bf16[512,3,2048]{0,1,2:T(4,128)(2,1)}), bf16[512,3,2048]{0,1,2:T(4,128)(2,1)}, u32[]{:S(2)}, u32[]{:S(2)}) async-start(bf16[512,3,2048]{0,1,2:T(4,128)(2,1)} %copy.35), calls=%async_computation | async-start | bytes 16777216 | tf_op jit(solution)/shard_map/all_to_all | solution.py:49
  32.0 530.7 %all-gather.2.cloned.1.call-start = ((), (), s32[]{:S(2)}) async-start(), calls=%async_computation.2 | async-start | bytes 20971520 | tf_op jit(solution)/shard_map/all_gather | solution.py:63
  249.4 7.0 slice-start
  272.8 6.9 copy-start
  290.3 5.7 copy-start
  306.7 5.7 copy-start
  323.1 8.4 copy-start
  349.6 5.7 copy-start.1
  367.3 5.7 copy-start.1
  385.0 5.7 copy-start.1
  402.7 5.7 copy-start.1
  420.6 72.8 %copy-start.9 = (bf16[2048,4,64]{0,2,1:T(8,128)(2,1)S(1)}, bf16[2048,4,64]{0,2,1:T(8,128)(2,1)}, u32[]{:S(2)}) copy-start(bf16[2048,4,64]{0,2,1:T(8,128)(2,1)} %copy-done.8) | copy-start | bytes 3145732
  420.6 72.8 %copy-start.11 = (bf16[2048,4,64]{0,2,1:T(8,128)(2,1)S(1)}, bf16[2048,4,64]{0,2,1:T(8,128)(2,1)}, u32[]{:S(2)}) copy-start(bf16[2048,4,64]{0,2,1:T(8,128)(2,1)} %copy-done.10) | copy-start | bytes 3145732
  424.7 5.7 copy-start.2
  442.4 5.7 copy-start.2
  460.1 5.7 copy-start.2
  477.8 5.7 copy-start.2
  496.8 5.7 copy-start.3
  514.2 5.7 copy-start.3
  531.5 5.7 copy-start.3
  548.8 5.7 copy-start.3
  562.8 6.7 copy-start.32
  562.8 6.7 copy-start.34
  576.7 5.7 copy-start.4
  595.9 5.7 copy-start.4
  615.1 5.7 copy-start.4
  634.3 5.7 copy-start.4
  651.5 66.0 %copy-start.21 = (f32[4,4,512]{2,1,0:T(4,128)S(1)}, f32[4,4,512]{2,1,0:T(4,128)}, u32[]{:S(2)}) copy-start(f32[4,4,512]{2,1,0:T(4,128)} %copy-done.20) | copy-start | bytes 98308
  651.6 66.0 %copy-start.23 = (f32[4,4,512]{2,1,0:T(4,128)S(1)}, f32[4,4,512]{2,1,0:T(4,128)}, u32[]{:S(2)}) copy-start(f32[4,4,512]{2,1,0:T(4,128)} %copy-done.22) | copy-start | bytes 98308
  651.6 66.0 %copy-start.25 = (f32[4,4,512]{2,1,0:T(4,128)S(1)}, f32[4,4,512]{2,1,0:T(4,128)}, u32[]{:S(2)}) copy-start(f32[4,4,512]{2,1,0:T(4,128)} %copy-done.24) | copy-start | bytes 98308
  651.6 66.0 %copy-start.27 = (f32[4,4,512]{2,1,0:T(4,128)S(1)}, f32[4,4,512]{2,1,0:T(4,128)}, u32[]{:S(2)}) copy-start(f32[4,4,512]{2,1,0:T(4,128)} %copy-done.26) | copy-start | bytes 98308
  654.1 5.7 copy-start.5
  670.5 5.7 copy-start.5
  686.8 5.7 copy-start.5
  703.2 5.7 copy-start.5
  717.6 7.2 copy-start.16
  717.6 7.2 copy-start.17
  731.7 5.7 copy-start.6
  750.9 5.7 copy-start.6
  789.3 5.7 copy-start.6
  806.5 65.7 %copy-start.29 = (f32[4,4,512]{2,1,0:T(4,128)S(1)}, f32[4,4,512]{2,1,0:T(4,128)}, u32[]{:S(2)}) copy-start(f32[4,4,512]{2,1,0:T(4,128)} %copy-done.28) | copy-start | bytes 98308
  806.5 65.7 %copy-start.31 = (f32[4,4,512]{2,1,0:T(4,128)S(1)}, f32[4,4,512]{2,1,0:T(4,128)}, u32[]{:S(2)}) copy-start(f32[4,4,512]{2,1,0:T(4,128)} %copy-done.30) | copy-start | bytes 98308
  806.5 65.7 %copy-start.33 = (f32[4,4,512]{2,1,0:T(4,128)S(1)}, f32[4,4,512]{2,1,0:T(4,128)}, u32[]{:S(2)}) copy-start(f32[4,4,512]{2,1,0:T(4,128)} %copy-done.32) | copy-start | bytes 98308
  806.5 65.7 %copy-start.35 = (f32[4,4,512]{2,1,0:T(4,128)S(1)}, f32[4,4,512]{2,1,0:T(4,128)}, u32[]{:S(2)}) copy-start(f32[4,4,512]{2,1,0:T(4,128)} %copy-done.34) | copy-start | bytes 98308
  825.5 5.7 copy-start.7
  841.9 5.7 copy-start.7
  858.3 5.7 copy-start.7
  872.2 6.1 copy-start.18
  (15 other events, 59.6 us)
Sparse Core Ops, SparseCore 0:
  260.5 156.6 all-gather.1
where the time goes:
time: 954 us; the launch traced here: 946 us
  matrix products  378 us (40%)
  local copies, waits for them, and re-layouts  196 us (21%)
  waiting for transfers between devices  183 us (19%)
  other arithmetic  115 us (12%)
  blocking collectives  52.2 us (5%)
  between operations  14 us (1%)
    dot_general x32, matrix products, one_tile(): jnp.einsum('hqk,khd->hqd', probs, values, preferred_element_type=jnp.floa...  275 us
    all_to_all x1, waiting for transfers between devices, on_device(): lax.all_to_all(shaped, 'head', split_axis=2, concat_axis=0, tiled=True)  183 us
    reduce_sum x32, other arithmetic, one_tile(): total = jnp.sum(probs.astype(jnp.float32), axis=-1)  105 us
    dot_general x32, matrix products, one_tile(): jnp.einsum('qhd,khd->hqk', query_tile, keys, preferred_element_type=jnp.f...  103 us
    while x64, local copies, waits for them, and re-layouts  82.2 us
    all_to_all x1, blocking collectives, on_device(): lax.all_to_all(outputs, 'head', split_axis=0, concat_axis=1, tiled=True)  52.2 us
    unnamed x60, local copies, waits for them, and re-layouts  21.4 us
  transfers between devices with their start and end apart: 2, of which 1 were waited for; matrix products, arithmetic and copies ran while one was open for 27% of the time, Pallas kernels for 0%

commit v1 on v0

v1 whole, which is shorter than its diff:
```python
import functools

import jax
import jax.numpy as jnp
from jax import lax
from jax.experimental import pallas as pl
from jax.experimental.pallas import tpu as pltpu
from jax.sharding import PartitionSpec as P

HEAD_DIM = 64
LANES = 128
BLOCK = 2048
HEAD_ROWS = 80
LIMIT = 1e30
F32 = jnp.float32
BF16 = jnp.bfloat16
NT = (((1,), (1,)), ((), ()))
ANY = pl.BlockSpec(memory_space=pl.ANY)


def params(mib=40):
    return pltpu.CompilerParams(vmem_limit_bytes=mib << 20)


def cost(units):
    return pl.CostEstimate(flops=int(units * 1e10), bytes_accessed=1 << 20, transcendentals=0)


def staged(moves, buf_ref, in_sem, out_sem):
    reads = [pltpu.make_async_copy(s, buf_ref.at[n], in_sem) for n, (s, _) in enumerate(moves)]
    writes = [pltpu.make_async_copy(buf_ref.at[n], d, out_sem) for n, (_, d) in enumerate(moves)]
    for copy in reads:
        copy.start()
    for copy in reads:
        copy.wait()
    for copy in writes:
        copy.start()
    for copy in writes:
        copy.wait()


def move(kernel, rank, arrays, out_shape, n, rows, units, aliases=None):
    many = isinstance(out_shape, list)
    n_in, n_out = len(arrays), len(out_shape) if many else 1

    def body(rank_ref, *refs):
        ins, outs, rest = refs[:n_in], refs[n_in : n_in + n_out], refs[n_in + n_out :]
        staged(kernel(rank_ref[0], ins, outs), *rest)

    return pl.pallas_call(
        body,
        in_specs=[pl.BlockSpec(memory_space=pltpu.SMEM)] + [ANY] * n_in,
        out_specs=[ANY] * n_out if many else ANY,
        out_shape=out_shape,
        scratch_shapes=[
            pltpu.VMEM((n, rows, LANES), BF16),
            pltpu.SemaphoreType.DMA,
            pltpu.SemaphoreType.DMA,
        ],
        input_output_aliases=aliases or {},
        compiler_params=params(),
        cost_estimate=cost(units),
    )(rank, *arrays)


def pack(rank, qkv, first, groups, order):
    rows = qkv.shape[0]
    width = qkv.shape[1] // 3

    def kernel(me, ins, outs):
        moves = []
        for out, (kinds, dest) in zip(outs, order):
            for at, k in enumerate(dest):
                owner = k if isinstance(k, int) else jnp.bitwise_xor(me, k[0])
                start = pl.multiple_of(owner * (width // groups) + first * LANES, LANES)
                for n, kind in enumerate(kinds):
                    moves.append((ins[0].at[:, pl.ds(kind * width + start, LANES)], out.at[at, n]))
        return moves

    shapes = [(len(dest), len(kinds), rows, LANES) for kinds, dest in order]
    n = sum(shape[0] * shape[1] for shape in shapes)
    shapes = [jax.ShapeDtypeStruct(shape, BF16) for shape in shapes]
    return move(kernel, rank, [qkv], shapes, n, rows, 0.2)


def merge(rank, pieces):
    rows, n = pieces[0].shape[2], len(pieces)

    def kernel(me, ins, outs):
        q, kv = outs
        moves = [(ins[k].at[0, 1 + i], kv.at[k, i]) for k in range(n) for i in range(2)]
        return moves + [(ins[k].at[0, 0], q.at[jnp.bitwise_xor(me, k)]) for k in range(n)]

    shapes = [(n, rows, LANES), (n, 2, rows, LANES)]
    shapes = [jax.ShapeDtypeStruct(shape, BF16) for shape in shapes]
    return move(kernel, rank, pieces, shapes, 3 * n, rows, 0.2)


def regroup(rank, arrays):
    groups, rows, _ = arrays[0].shape
    n = len(arrays)

    def kernel(me, ins, outs):
        return [
            (ins[p].at[jnp.bitwise_xor(me, k)], out.at[p])
            for k, out in enumerate(outs)
            for p in range(n)
        ]

    shapes = [jax.ShapeDtypeStruct((n, rows, LANES), BF16)] * groups
    return move(kernel, rank, arrays, shapes, n * groups, rows, 0.2)


def place_early(rank, pieces, shape):
    n, rows, _ = pieces[0].shape
    width = shape[1] // len(pieces)

    def kernel(me, ins, outs):
        moves = []
        for k, piece in enumerate(ins):
            for p in range(n):
                start = pl.multiple_of(jnp.bitwise_xor(me, k) * width + p * LANES, LANES)
                moves.append((piece.at[p], outs[0].at[:, pl.ds(start, LANES)]))
        return moves

    out = jax.ShapeDtypeStruct(shape, BF16)
    return move(kernel, rank, pieces, out, n * len(pieces), rows, 0.2)


def place_last(rank, pieces, base, pair):
    groups, rows, _ = pieces.shape
    width = base.shape[1] // groups

    def kernel(me, ins, outs):
        return [
            (ins[0].at[k], outs[0].at[:, pl.ds(k * width + pair * LANES, LANES)])
            for k in range(groups)
        ]

    out = jax.ShapeDtypeStruct(base.shape, BF16)
    return move(kernel, rank, [pieces, base], out, groups, rows, 0.1, {2: 0})


def prepare(kv_refs, keys_ref, values_ref):
    tokens = keys_ref.shape[2]
    rows = kv_refs[0].shape[2]
    pieces = [(ref, g) for ref in kv_refs for g in range(ref.shape[0])]
    for n, (kv_ref, g) in enumerate(pieces):
        slot, at = divmod(n * rows, tokens)
        keys = kv_ref[g, 0]
        lane = lax.broadcasted_iota(jnp.int32, keys.shape, 1)
        one = jnp.ones_like(keys)
        span = pl.ds(at, rows)
        keys_ref[slot, 0, span, :] = jnp.where(lane < HEAD_DIM, keys, one)
        keys_ref[slot, 1, span, :] = jnp.where(lane < HEAD_DIM, one, keys)
        values = kv_ref[g, 1].T
        for h in range(2):
            values_ref[slot, h, :HEAD_DIM, span] = values[h * HEAD_DIM : (h + 1) * HEAD_DIM]
            values_ref[slot, h, HEAD_DIM:, span] = jnp.ones((HEAD_ROWS - HEAD_DIM, rows), BF16)


def weigh(keys, values, query):
    scores = lax.dot_general(keys, query, NT, preferred_element_type=F32)
    probs = jnp.exp(scores).astype(BF16)
    return jnp.dot(values, probs, preferred_element_type=F32)


def first_kernel(q_ref, kv_ref, qe_ref, acc_ref, keys_ref, values_ref):
    h = pl.program_id(1)

    @pl.when((pl.program_id(0) == 0) & (h == 0))
    def _():
        prepare([kv_ref], keys_ref, values_ref)

    query = q_ref[...] * jnp.asarray(HEAD_DIM**-0.5, BF16)
    lane = lax.broadcasted_iota(jnp.int32, query.shape, 1)
    mine = (lane // HEAD_DIM) == h
    query = jnp.where(mine, query, jnp.zeros_like(query))
    probe = 256
    some = lax.dot_general(query, keys_ref[0, h, :probe, :], NT, preferred_element_type=F32)
    shift = -jnp.max(some, axis=1, keepdims=True)
    query = jnp.where(lane == (1 - h) * HEAD_DIM, shift.astype(BF16), query)
    qe_ref[0] = query
    acc_ref[0] = weigh(keys_ref[0, h], values_ref[0, h], query)


def first(q, kv):
    tokens = q.shape[0] * q.shape[1]
    tile = min(512, tokens)
    return pl.pallas_call(
        first_kernel,
        grid=(tokens // tile, 2),
        in_specs=[
            pl.BlockSpec((tile, LANES), lambda i, h: (i, 0)),
            pl.BlockSpec(kv.shape, lambda i, h: (0, 0, 0, 0)),
        ],
        out_specs=[
            pl.BlockSpec((1, tile, LANES), lambda i, h: (h, i, 0)),
            pl.BlockSpec((1, HEAD_ROWS, tile), lambda i, h: (h, 0, i)),
        ],
        out_shape=[
            jax.ShapeDtypeStruct((2, tokens, LANES), BF16),
            jax.ShapeDtypeStruct((2, HEAD_ROWS, tokens), F32),
        ],
        scratch_shapes=[
            pltpu.VMEM((1, 2, tokens, LANES), BF16),
            pltpu.VMEM((1, 2, HEAD_ROWS, tokens), BF16),
        ],
        compiler_params=params(),
        cost_estimate=cost(1),
    )(q.reshape(tokens, LANES), kv)


def blocks_of(kvs, tokens):
    return sum(kv.shape[0] * kv.shape[2] for kv in kvs) // tokens


def more_kernel(qe_ref, acc_ref, *refs, n_refs, n):
    kv_refs, (out_ref, keys_ref, values_ref) = refs[:n_refs], refs[n_refs:]
    h = pl.program_id(1)

    @pl.when((pl.program_id(0) == 0) & (h == 0))
    def _():
        prepare(kv_refs, keys_ref, values_ref)

    query = qe_ref[0]
    out_ref[0] = acc_ref[0]

    def step(slot, carry):
        out_ref[0] += weigh(keys_ref[slot, h], values_ref[slot, h], query)
        return carry

    lax.fori_loop(0, n, step, 0)


def more(qe, acc, kvs):
    tokens = qe.shape[1]
    n = blocks_of(kvs, tokens)
    tile = min(512, tokens)
    state = pl.BlockSpec((1, HEAD_ROWS, tile), lambda i, h: (h, 0, i))
    return pl.pallas_call(
        functools.partial(more_kernel, n_refs=len(kvs), n=n),
        grid=(tokens // tile, 2),
        in_specs=[pl.BlockSpec((1, tile, LANES), lambda i, h: (h, i, 0)), state]
        + [pl.BlockSpec(kv.shape, lambda i, h: (0, 0, 0, 0)) for kv in kvs],
        out_specs=state,
        out_shape=jax.ShapeDtypeStruct(acc.shape, F32),
        scratch_shapes=[
            pltpu.VMEM((n, 2, tokens, LANES), BF16),
            pltpu.VMEM((n, 2, HEAD_ROWS, tokens), BF16),
        ],
        input_output_aliases={1: 0},
        compiler_params=params(),
        cost_estimate=cost(n),
    )(qe, acc, *kvs)


def last_kernel(qe_ref, acc_ref, *refs, n_refs, n_all, n):
    kv_refs, all_refs = refs[:n_refs], refs[n_refs : n_refs + n_all]
    out_ref, keys_ref, values_ref, sum_ref, both_ref, buf_ref, sem = refs[n_refs + n_all :]
    h = pl.program_id(1)

    @pl.when((pl.program_id(0) == 0) & (h == 0))
    def _():
        prepare(kv_refs, keys_ref, values_ref)

    query = qe_ref[0]
    sum_ref[...] = acc_ref[0]

    def step(slot, carry):
        sum_ref[...] += weigh(keys_ref[slot, h], values_ref[slot, h], query)
        return carry

    lax.fori_loop(0, n, step, 0)
    safe = jnp.max(jnp.where(sum_ref[HEAD_DIM : HEAD_DIM + 1, :] < LIMIT, 0.0, 1.0)) == 0.0

    @pl.when(jnp.logical_not(safe))
    def _():
        lane = lax.broadcasted_iota(jnp.int32, query.shape, 1)
        plain = jnp.where((lane // HEAD_DIM) == h, query, jnp.zeros_like(query))
        rows = buf_ref.shape[1]
        pieces = [(ref, g) for ref in all_refs for g in range(ref.shape[0])]
        sum_ref[...] = jnp.zeros_like(sum_ref)

        def piece(at, top):
            for index, (ref, g) in enumerate(pieces):

                @pl.when(at == index)
                def _(ref=ref, g=g):
                    copy = pltpu.make_async_copy(ref.at[g], buf_ref, sem)
                    copy.start()
                    copy.wait()

            scores = lax.dot_general(buf_ref[0], plain, NT, preferred_element_type=F32)
            higher = jnp.maximum(top, jnp.max(scores, axis=0, keepdims=True))
            probs = jnp.exp(scores - higher).astype(BF16)
            values = buf_ref[1].T
            values = jnp.where(h == 0, values[:HEAD_DIM], values[HEAD_DIM:])
            ones = jnp.ones((HEAD_ROWS - HEAD_DIM, rows), BF16)
            values = jnp.concatenate([values, ones], axis=0)
            part = jnp.dot(values, probs, preferred_element_type=F32)
            sum_ref[...] = sum_ref[...] * jnp.exp(top - higher) + part
            return higher

        lax.fori_loop(0, len(pieces), piece, jnp.full((1, query.shape[0]), -1e30, F32))

    both_ref[h] = sum_ref[:HEAD_DIM, :] / sum_ref[HEAD_DIM : HEAD_DIM + 1, :]

    @pl.when(h == 1)
    def _():
        joined = jnp.concatenate([both_ref[0], both_ref[1]], axis=0)
        out_ref[...] = joined.T.astype(BF16)


def last(qe, acc, kvs, all_kvs):
    n_all = len(all_kvs)
    tokens = qe.shape[1]
    n = blocks_of(kvs, tokens)
    tile = min(512, tokens)
    rows = kvs[0].shape[2]
    out = pl.pallas_call(
        functools.partial(last_kernel, n_refs=len(kvs), n_all=n_all, n=n),
        grid=(tokens // tile, 2),
        in_specs=[
            pl.BlockSpec((1, tile, LANES), lambda i, h: (h, i, 0)),
            pl.BlockSpec((1, HEAD_ROWS, tile), lambda i, h: (h, 0, i)),
        ]
        + [pl.BlockSpec(kv.shape, lambda i, h: (0, 0, 0, 0)) for kv in kvs]
        + [ANY] * n_all,
        out_specs=pl.BlockSpec((tile, LANES), lambda i, h: (i, 0)),
        out_shape=jax.ShapeDtypeStruct((tokens, LANES), BF16),
        scratch_shapes=[
            pltpu.VMEM((n, 2, tokens, LANES), BF16),
            pltpu.VMEM((n, 2, HEAD_ROWS, tokens), BF16),
            pltpu.VMEM((HEAD_ROWS, tile), F32),
            pltpu.VMEM((2, HEAD_DIM, tile), F32),
            pltpu.VMEM((2, rows, LANES), BF16),
            pltpu.SemaphoreType.DMA,
        ],
        compiler_params=params(),
        cost_estimate=cost(n),
    )(qe, acc, *kvs, *all_kvs)
    return out.reshape(tokens // rows, rows, LANES)


def swap(x, axis, bit):
    size = lax.axis_size(axis)
    return lax.ppermute(x, axis, [(i, i ^ bit) for i in range(size)])


def on_device(qkv):
    size = lax.axis_size("head")
    groups = size // 2
    rows = qkv.shape[0]
    width = qkv.shape[1] // 3
    pairs = width // groups // LANES
    bits = lax.axis_size("blk").bit_length() - 1
    rank = jnp.bitwise_and(lax.axis_index("head"), groups - 1).astype(jnp.int32).reshape(1)
    teams = [list(range(groups)), list(range(groups, size))]
    ranks = tuple(range(groups))

    def exchange(x):
        return lax.all_to_all(
            x, "head", split_axis=0, concat_axis=0, tiled=True, axis_index_groups=teams
        )

    order = [((1, 2), ranks), ((0,), ranks)] + [((1, 2), ((k,),)) for k in range(groups)]
    kv_all, q_all, *direct = pack(rank, qkv, 0, groups, order)
    far = [[swap(direct[k], "head", groups ^ k) for k in range(groups)]]
    own = [exchange(kv_all)]
    query = [exchange(q_all)[:, 0]]
    near = [[swap(own[0], "blk", 1 << bit) for bit in range(bits)]]
    for p in range(1, pairs):
        pieces = pack(rank, qkv, p, groups, [((0, 1, 2), ((k,),)) for k in range(groups)])
        pieces = [pieces[0]] + [swap(pieces[k], "head", k) for k in range(1, groups)]
        q, kv = merge(rank, pieces)
        query.append(q)
        own.append(kv)
        far.append([swap(kv, "head", groups)])
        near.append([swap(kv, "blk", 1 << bit) for bit in range(bits)])

    states = [first(query[p], own[p]) for p in range(pairs)]
    outs = []
    for p in range(pairs):
        qe, acc = states[p]
        everything = [own[p]] + near[p] + far[p]
        if p < pairs - 1:
            outs.append(last(qe, acc, near[p] + far[p], everything))
        else:
            acc = more(qe, acc, near[p])
            outs.append(last(qe, acc, far[p], everything))
    early = regroup(rank, outs[:-1])
    early = [early[0]] + [swap(early[k], "head", k) for k in range(1, groups)]
    result = place_early(rank, early, (rows, width))
    return place_last(rank, exchange(outs[-1]), result, pairs - 1)


def solution(mesh):
    spec = P(("blk", "head"), None)
    return jax.shard_map(on_device, mesh=mesh, in_specs=(spec,), out_specs=spec, check_vma=False)
```

time: 954 us -> 824 us (0.86)
  Pallas kernels: 0 us -> 675 us
  matrix products: 378 us -> 0 us
  local copies, waits for them, and re-layouts: 196 us -> 17.7 us
  other arithmetic: 115 us -> 0 us
  waiting for transfers between devices: 183 us -> 85.1 us
  blocking collectives: 52.2 us -> 0 us
  starting transfers between devices: 6.38 us -> 40.7 us
  between operations: 14 us -> 0.55 us
    pallas_call x0 -> x19, Pallas kernels: none -> 675 us  [the longest x4 583 us: last(): pl.pallas_call(functools.partial(last_kernel, n_refs=len(kvs), n_all=n_al...]
    dot_general x64 -> x0, matrix products: 378 us -> none  [the longest x32 275 us: one_tile(): jnp.einsum('hqk,khd->hqd', probs, values, preferred_element_type=jnp.floa...]
    all_to_all x1 -> x3, waiting for transfers between devices: 183 us -> 0.01 us  [exchange(): lax.all_to_all(x, 'head', split_axis=0, concat_axis=0, tiled=True, axis_i...]
    reduce_sum x32 -> x0, other arithmetic: 105 us -> none  [one_tile(): total = jnp.sum(probs.astype(jnp.float32), axis=-1)]
    ppermute x0 -> x27, waiting for transfers between devices: none -> 85.1 us  [swap(): return lax.ppermute(x, axis, [(i, i ^ bit) for i in range(size)])]
    while x64 -> x0, local copies, waits for them, and re-layouts: 82.2 us -> none
    all_to_all x1 -> x0, blocking collectives: 52.2 us -> none  [on_device(): lax.all_to_all(outputs, 'head', split_axis=0, concat_axis=1, tiled=True)]
    ppermute x0 -> x27, starting transfers between devices: none -> 27.6 us  [swap(): return lax.ppermute(x, axis, [(i, i ^ bit) for i in range(size)])]
  transfers between devices with their start and end apart: 2 -> 30, of which waited for: 1 -> 8; matrix products, arithmetic and copies ran while one was open for 27% -> 0% of each run, Pallas kernels for 0% -> 82%
where the time goes in v1:
time: 824 us; the launch traced here: 819 us
  Pallas kernels  675 us (82%)
  waiting for transfers between devices  85.1 us (10%)
  starting transfers between devices  40.7 us (5%)
  local copies, waits for them, and re-layouts  17.7 us (2%)
    pallas_call x4, Pallas kernels, last(): pl.pallas_call(functools.partial(last_kernel, n_refs=len(kvs), n_all=n_al...  583 us
    ppermute x27, waiting for transfers between devices, swap(): return lax.ppermute(x, axis, [(i, i ^ bit) for i in range(size)])  85.1 us
    pallas_call x4, Pallas kernels, first(): pl.pallas_call(first_kernel, grid=(tokens // tile, 2), in_specs=[pl.Block...  44.6 us
    pallas_call x10, Pallas kernels, move(): pl.pallas_call(body, in_specs=[pl.BlockSpec(memory_space=pltpu.SMEM)] + [...  29.9 us
    ppermute x27, starting transfers between devices, swap(): return lax.ppermute(x, axis, [(i, i ^ bit) for i in range(size)])  27.6 us
    pallas_call x1, Pallas kernels, more(): pl.pallas_call(functools.partial(more_kernel, n_refs=len(kvs), n=n), grid...  18 us
    unnamed x40, local copies, waits for them, and re-layouts  17.7 us
  transfers between devices with their start and end apart: 30, of which 8 were waited for; matrix products, arithmetic and copies ran while one was open for 0% of the time, Pallas kernels for 82%

profile of v1, /device:TPU:1, one launch (start us, length us, event | category | flops | bytes accessed | tf_op | source)
XLA Modules:
  0.0 819.4 jit_solution(2158568304003816382)
XLA Ops:
  0.0 2.8 copy-done
  2.8 2.0 shard_map.17
  5.6 2.7 collective-permute-start.1
  8.3 2.2 shard_map.22
  11.3 3.9 all-to-all-start.2
  15.2 2.5 collective-permute-start.8
  17.8 2.8 copy-done.1
  20.6 2.5 shard_map.25
  23.1 2.5 shard_map.29
  25.9 1.6 collective-permute-start.13
  27.5 10.3 %collective-permute-done.2.refs_3_ = bf16[1,3,512,128]{3,2,1,0:T(8,128)(2,1)S(1)} collective-permute-done((bf16[1,3,512,128]{3,2,1,0:T(8,128)(2,1)S(1)}, bf16[1,3,512,128]{3,2,1,0:T(8,128)(2,1)S(1)}, u32[]{:S(2)}, u32[]{:S(2)}) %collective-permute-start.2) | collective-permute-done | bytes 393248 | tf_op jit(solution)/shard_map/ppermute | solution.py:348
  39.6 4.0 shard_map.18
  43.6 11.2 %shard_map.19 = (bf16[2,2048,128]{2,1,0:T(8,128)(2,1)S(1)}, f32[2,80,2048]{2,1,0:T(8,128)S(1)}) custom-call(bf16[2048,128]{1,0:T(8,128)(2,1)S(1)} %bitcast.13, bf16[4,2,512,128]{3,2,1,0:T(8,128)(2,1)S(1)} %get-tuple-element.46.kv_ref.refs_1_), custom_call_target="tpu_custom_call" | custom-call | flops 10000000000 | bytes 1048576 | tf_op jit(solution)/shard_map/pallas_call | solution.py:190
  54.9 2.2 collective-permute-done.13.refs_2_
  57.1 1.3 collective-permute-start.19
  58.4 7.2 collective-permute-done.14.refs_3_
  65.6 1.5 collective-permute-start.20
  67.1 4.0 shard_map.26
  71.1 11.2 %shard_map.27 = (bf16[2,2048,128]{2,1,0:T(8,128)(2,1)S(1)}, f32[2,80,2048]{2,1,0:T(8,128)S(1)}) custom-call(bf16[2048,128]{1,0:T(8,128)(2,1)S(1)} %bitcast.14, bf16[4,2,512,128]{3,2,1,0:T(8,128)(2,1)S(1)} %get-tuple-element.62.kv_ref.refs_3_), custom_call_target="tpu_custom_call" | custom-call | flops 10000000000 | bytes 1048576 | tf_op jit(solution)/shard_map/pallas_call | solution.py:190
  82.3 1.3 collective-permute-start.15
  83.6 1.3 collective-permute-start.16
  84.8 2.3 collective-permute-start.17
  87.1 4.0 shard_map.30
  91.2 11.2 %shard_map.31 = (bf16[2,2048,128]{2,1,0:T(8,128)(2,1)S(1)}, f32[2,80,2048]{2,1,0:T(8,128)S(1)}) custom-call(bf16[2048,128]{1,0:T(8,128)(2,1)S(1)} %bitcast.15, bf16[4,2,512,128]{3,2,1,0:T(8,128)(2,1)S(1)} %get-tuple-element.70.kv_ref.refs_3_), custom_call_target="tpu_custom_call" | custom-call | flops 10000000000 | bytes 1048576 | tf_op jit(solution)/shard_map/pallas_call | solution.py:190
  102.4 4.1 collective-permute-done.15.refs_0_.refs_4_
  107.7 1.3 collective-permute-start.22
  109.0 24.3 %collective-permute-done.17.refs_2_.refs_6_ = bf16[4,2,512,128]{3,2,1,0:T(8,128)(2,1)S(1)} collective-permute-done((bf16[4,2,512,128]{3,2,1,0:T(8,128)(2,1)S(1)}, bf16[4,2,512,128]{3,2,1,0:T(8,128)(2,1)S(1)}, u32[]{:S(2)}, u32[]{:S(2)}) %collective-permute-start.17) | collective-permute-done | bytes 1048608 | tf_op jit(solution)/shard_map/ppermute | solution.py:348
  133.2 123.1 %shard_map.28 = bf16[2048,128]{1,0:T(8,128)(2,1)S(1)} custom-call(bf16[2,2048,128]{2,1,0:T(8,128)(2,1)S(1)} %get-tuple-element.63.qe_ref, f32[2,80,2048]{2,1,0:T(8,128)S(1)} %get-tuple-element.64.acc_ref, bf16[4,2,512,128]{3,2,1,0:T(8,128)(2,1)S(1)} %collective-permute-done.15.refs_0_.refs_4_, ...), custom_call_target="tpu_custom_call" | custom-call | flops 30000001024 | bytes 1048576 | tf_op jit(solution)/shard_map/pallas_call | solution.py:321
  256.4 1.4 collective-permute-start.10
  258.0 1.6 collective-permute-start.4
  259.6 123.1 %shard_map.32 = bf16[2048,128]{1,0:T(8,128)(2,1)S(1)} custom-call(bf16[2,2048,128]{2,1,0:T(8,128)(2,1)S(1)} %get-tuple-element.71.qe_ref, f32[2,80,2048]{2,1,0:T(8,128)S(1)} %get-tuple-element.72.acc_ref, bf16[4,2,512,128]{3,2,1,0:T(8,128)(2,1)S(1)} %collective-permute-done.21.refs_0_.refs_4_, ...), custom_call_target="tpu_custom_call" | custom-call | flops 30000001024 | bytes 1048576 | tf_op jit(solution)/shard_map/pallas_call | solution.py:321
  383.6 1.5 collective-permute-start.5
  385.0 18.0 %shard_map.20.acc_ref = f32[2,80,2048]{2,1,0:T(8,128)S(1)} custom-call(bf16[2,2048,128]{2,1,0:T(8,128)(2,1)S(1)} %get-tuple-element.47.qe_ref, f32[2,80,2048]{2,1,0:T(8,128)S(1)} %get-tuple-element.48.acc_ref, bf16[4,2,512,128]{3,2,1,0:T(8,128)(2,1)S(1)} %collective-permute-done.3.refs_0_.refs_2_, ...), custom_call_target="tpu_custom_call", output_to_operand_aliasing={{}: (1, {})} | custom-call | flops 20000000000 | bytes 1048576 | tf_op jit(solution)/shard_map/pallas_call | solution.py:241
  406.2 5.7 all-to-all-start.1
  412.5 19.6 %collective-permute-done.5.refs_0_.refs_4_ = bf16[4,2,512,128]{3,2,1,0:T(8,128)(2,1)} collective-permute-done((bf16[4,2,512,128]{3,2,1,0:T(8,128)(2,1)S(1)}, bf16[4,2,512,128]{3,2,1,0:T(8,128)(2,1)}, u32[]{:S(2)}, u32[]{:S(2)}) %collective-permute-start.5) | collective-permute-done | bytes 1048608 | tf_op jit(solution)/shard_map/ppermute | solution.py:348
  432.1 1.2 copy-done.3
  434.5 1.3 copy-done.17
  437.1 135.1 %shard_map.21 = bf16[2048,128]{1,0:T(8,128)(2,1)} custom-call(bf16[2,2048,128]{2,1,0:T(8,128)(2,1)S(1)} %copy-done.19, f32[2,80,2048]{2,1,0:T(8,128)S(1)} %copy-done.17, bf16[4,2,512,128]{3,2,1,0:T(8,128)(2,1)} %collective-permute-done.5.refs_0_.refs_4_, bf16[4,2,512,128]{3,2,1,0:T(8,128)(2,1)S(1)} %get-tuple-element.46.kv_ref.refs_1_, ...), custom_call_target="tpu_custom_call" | custom-call | flops 10000000000 | bytes 1048576 | tf_op jit(solution)/shard_map/pallas_call | solution.py:321
  572.2 2.7 collective-permute-start.11
  574.9 3.5 all-to-all-start
  578.4 11.2 %shard_map.23 = (bf16[2,2048,128]{2,1,0:T(8,128)(2,1)S(1)}, f32[2,80,2048]{2,1,0:T(8,128)S(1)}) custom-call(bf16[2048,128]{1,0:T(8,128)(2,1)S(1)} %bitcast.9, bf16[4,2,512,128]{3,2,1,0:T(8,128)(2,1)S(1)} %all-to-all-done.2.kv_ref.refs_6_), custom_call_target="tpu_custom_call" | custom-call | flops 10000000000 | bytes 1048576 | tf_op jit(solution)/shard_map/pallas_call | solution.py:190
  589.6 201.5 %shard_map.24 = bf16[2048,128]{1,0:T(8,128)(2,1)S(1)} custom-call(bf16[2,2048,128]{2,1,0:T(8,128)(2,1)S(1)} %get-tuple-element.51.qe_ref, f32[2,80,2048]{2,1,0:T(8,128)S(1)} %get-tuple-element.52.acc_ref, bf16[4,2,512,128]{3,2,1,0:T(8,128)(2,1)} %collective-permute-done.6.refs_0_.refs_7_, bf16[4,2,512,128]{3,2,1,0:T(8,128)(2,1)} %collective-permute-done.7.refs_1_.refs_8_, ...), custom_call_target="tpu_custom_call" | custom-call | flops 30000001024 | bytes 1048576 | tf_op jit(solution)/shard_map/pallas_call | solution.py:321
  791.1 4.1 shard_map.33
  796.0 1.4 collective-permute-start.26
  797.4 8.2 collective-permute-done.25.refs_2_
  805.6 9.0 %collective-permute-done.26.refs_3_ = bf16[3,512,128]{2,1,0:T(8,128)(2,1)S(1)} collective-permute-done((bf16[3,512,128]{2,1,0:T(8,128)(2,1)S(1)}, bf16[3,512,128]{2,1,0:T(8,128)(2,1)S(1)}, u32[]{:S(2)}, u32[]{:S(2)}) %collective-permute-start.26) | collective-permute-done | bytes 393248 | tf_op jit(solution)/shard_map/ppermute | solution.py:348
  814.6 3.1 shard_map.34.refs_1_
  817.8 1.5 shard_map.35
  (71 shorter events, 13.1 us)
Async XLA Ops:
  0.0 2.8 copy-start
  4.8 0.8 copy-start.14
  5.5 20.1 %collective-permute-start = (bf16[1,3,512,128]{3,2,1,0:T(8,128)(2,1)}, bf16[1,3,512,128]{3,2,1,0:T(8,128)(2,1)S(1)}, u32[]{:S(2)}, u32[]{:S(2)}) collective-permute-start(bf16[1,3,512,128]{3,2,1,0:T(8,128)(2,1)} %get-tuple-element.42), channel_id=1, source_target_pairs={{0,1},{1,0},{2,3},{3,2},{4,5},{5,4},{6,7},{7,6},{8,9},{9,8},{10,11... | collective-permute-start | bytes 1179656 | tf_op jit(solution)/shard_map/ppermute | solution.py:348
  5.6 20.3 %collective-permute-start.1 = (bf16[1,3,512,128]{3,2,1,0:T(8,128)(2,1)S(1)}, bf16[1,3,512,128]{3,2,1,0:T(8,128)(2,1)S(1)}, u32[]{:S(2)}, u32[]{:S(2)}) collective-permute-start(bf16[1,3,512,128]{3,2,1,0:T(8,128)(2,1)S(1)} %get-tuple-element.43), channel_id=1, source_target_pairs={{0,2},{1,3},{2,0},{3,1},{4,6},{5,7},{6,4},{7,5},{8,10},{9,11},{10,... | collective-permute-start | bytes 1179656 | tf_op jit(solution)/shard_map/ppermute | solution.py:348
  8.3 29.5 %collective-permute-start.2 = (bf16[1,3,512,128]{3,2,1,0:T(8,128)(2,1)S(1)}, bf16[1,3,512,128]{3,2,1,0:T(8,128)(2,1)S(1)}, u32[]{:S(2)}, u32[]{:S(2)}) collective-permute-start(bf16[1,3,512,128]{3,2,1,0:T(8,128)(2,1)S(1)} %get-tuple-element.44), channel_id=1, source_target_pairs={{0,3},{1,2},{2,1},{3,0},{4,7},{5,6},{6,5},{7,4},{8,11},{9,10},{10,... | collective-permute-start | bytes 1179656 | tf_op jit(solution)/shard_map/ppermute | solution.py:348
  11.3 394.9 %all-to-all-start.2 = ((bf16[4,2,512,128]{3,2,1,0:T(8,128)(2,1)}), bf16[4,2,512,128]{3,2,1,0:T(8,128)(2,1)S(1)}, u32[]{:S(2)}, u32[]{:S(2)}) async-start(bf16[4,2,512,128]{3,2,1,0:T(8,128)(2,1)} %get-tuple-element.50), calls=%async_computation.2 | async-start | bytes 2097152 | tf_op jit(solution)/shard_map/all_to_all | solution.py:363
  15.2 557.0 %collective-permute-start.8 = (bf16[1,2,512,128]{3,2,1,0:T(8,128)(2,1)}, bf16[1,2,512,128]{3,2,1,0:T(8,128)(2,1)}, u32[]{:S(2)}, u32[]{:S(2)}) collective-permute-start(bf16[1,2,512,128]{3,2,1,0:T(8,128)(2,1)} %get-tuple-element.53), channel_id=1, source_target_pairs={{0,4},{1,5},{2,6},{3,7},{4,0},{5,1},{6,2},{7,3},{8,12},{9,13},{10,... | collective-permute-start | bytes 786440 | tf_op jit(solution)/shard_map/ppermute | solution.py:348
  17.7 571.9 %collective-permute-start.9 = (bf16[1,2,512,128]{3,2,1,0:T(8,128)(2,1)}, bf16[1,2,512,128]{3,2,1,0:T(8,128)(2,1)}, u32[]{:S(2)}, u32[]{:S(2)}) collective-permute-start(bf16[1,2,512,128]{3,2,1,0:T(8,128)(2,1)} %get-tuple-element.54), channel_id=1, source_target_pairs={{0,5},{1,4},{2,7},{3,6},{4,1},{5,0},{6,3},{7,2},{8,13},{9,12},{10,... | collective-permute-start | bytes 786440 | tf_op jit(solution)/shard_map/ppermute | solution.py:348
  17.8 2.8 copy-start.1
  23.1 15.5 %copy-start.15 = (bf16[1,3,512,128]{3,2,1,0:T(8,128)(2,1)S(1)}, bf16[1,3,512,128]{3,2,1,0:T(8,128)(2,1)}, u32[]{:S(2)}) copy-start(bf16[1,3,512,128]{3,2,1,0:T(8,128)(2,1)} %copy-done.14) | copy-start | bytes 1179652
  25.6 29.2 %collective-permute-start.12 = (bf16[1,3,512,128]{3,2,1,0:T(8,128)(2,1)S(1)}, bf16[1,3,512,128]{3,2,1,0:T(8,128)(2,1)S(1)}, u32[]{:S(2)}, u32[]{:S(2)}) collective-permute-start(bf16[1,3,512,128]{3,2,1,0:T(8,128)(2,1)S(1)} %get-tuple-element.58), channel_id=1, source_target_pairs={{0,1},{1,0},{2,3},{3,2},{4,5},{5,4},{6,7},{7,6},{8,9},{9,8},{10,11... | collective-permute-start | bytes 1179656 | tf_op jit(solution)/shard_map/ppermute | solution.py:348
  25.9 31.2 %collective-permute-start.13 = (bf16[1,3,512,128]{3,2,1,0:T(8,128)(2,1)S(1)}, bf16[1,3,512,128]{3,2,1,0:T(8,128)(2,1)S(1)}, u32[]{:S(2)}, u32[]{:S(2)}) collective-permute-start(bf16[1,3,512,128]{3,2,1,0:T(8,128)(2,1)S(1)} %get-tuple-element.59), channel_id=1, source_target_pairs={{0,2},{1,3},{2,0},{3,1},{4,6},{5,7},{6,4},{7,5},{8,10},{9,11},{10,... | collective-permute-start | bytes 1179656 | tf_op jit(solution)/shard_map/ppermute | solution.py:348
  38.6 27.0 %collective-permute-start.14 = (bf16[1,3,512,128]{3,2,1,0:T(8,128)(2,1)S(1)}, bf16[1,3,512,128]{3,2,1,0:T(8,128)(2,1)S(1)}, u32[]{:S(2)}, u32[]{:S(2)}) collective-permute-start(bf16[1,3,512,128]{3,2,1,0:T(8,128)(2,1)S(1)} %get-tuple-element.60), channel_id=1, source_target_pairs={{0,3},{1,2},{2,1},{3,0},{4,7},{5,6},{6,5},{7,4},{8,11},{9,10},{10,... | collective-permute-start | bytes 1179656 | tf_op jit(solution)/shard_map/ppermute | solution.py:348
  38.6 1.0 copy-start.7
  54.8 330.2 %copy-start.18 = (bf16[2,2048,128]{2,1,0:T(8,128)(2,1)}, bf16[2,2048,128]{2,1,0:T(8,128)(2,1)S(1)}, u32[]{:S(2)}) copy-start(bf16[2,2048,128]{2,1,0:T(8,128)(2,1)S(1)} %get-tuple-element.47.qe_ref) | copy-start | bytes 3145732
  54.8 27.5 %collective-permute-start.18 = (bf16[1,3,512,128]{3,2,1,0:T(8,128)(2,1)S(1)}, bf16[1,3,512,128]{3,2,1,0:T(8,128)(2,1)S(1)}, u32[]{:S(2)}, u32[]{:S(2)}) collective-permute-start(bf16[1,3,512,128]{3,2,1,0:T(8,128)(2,1)S(1)} %get-tuple-element.66), channel_id=1, source_target_pairs={{0,1},{1,0},{2,3},{3,2},{4,5},{5,4},{6,7},{7,6},{8,9},{9,8},{10,11... | collective-permute-start | bytes 1179656 | tf_op jit(solution)/shard_map/ppermute | solution.py:348
  57.1 26.5 %collective-permute-start.19 = (bf16[1,3,512,128]{3,2,1,0:T(8,128)(2,1)S(1)}, bf16[1,3,512,128]{3,2,1,0:T(8,128)(2,1)S(1)}, u32[]{:S(2)}, u32[]{:S(2)}) collective-permute-start(bf16[1,3,512,128]{3,2,1,0:T(8,128)(2,1)S(1)} %get-tuple-element.67), channel_id=1, source_target_pairs={{0,2},{1,3},{2,0},{3,1},{4,6},{5,7},{6,4},{7,5},{8,10},{9,11},{10,... | collective-permute-start | bytes 1179656 | tf_op jit(solution)/shard_map/ppermute | solution.py:348
  65.6 19.2 %collective-permute-start.20 = (bf16[1,3,512,128]{3,2,1,0:T(8,128)(2,1)S(1)}, bf16[1,3,512,128]{3,2,1,0:T(8,128)(2,1)S(1)}, u32[]{:S(2)}, u32[]{:S(2)}) collective-permute-start(bf16[1,3,512,128]{3,2,1,0:T(8,128)(2,1)S(1)} %get-tuple-element.68), channel_id=1, source_target_pairs={{0,3},{1,2},{2,1},{3,0},{4,7},{5,6},{6,5},{7,4},{8,11},{9,10},{10,... | collective-permute-start | bytes 1179656 | tf_op jit(solution)/shard_map/ppermute | solution.py:348
  82.3 24.2 %collective-permute-start.15 = (bf16[4,2,512,128]{3,2,1,0:T(8,128)(2,1)S(1)}, bf16[4,2,512,128]{3,2,1,0:T(8,128)(2,1)S(1)}, u32[]{:S(2)}, u32[]{:S(2)}) collective-permute-start(bf16[4,2,512,128]{3,2,1,0:T(8,128)(2,1)S(1)} %get-tuple-element.62.kv_ref.refs_3_), channel_id=1, source_target_pairs={{0,8},{8,0},{16,24},{24,16},{1,9},{9,1},{17,25},{25,17},{2,10},{10... | collective-permute-start | bytes 3145736 | tf_op jit(solution)/shard_map/ppermute | solution.py:348
  83.6 24.1 %collective-permute-start.16 = (bf16[4,2,512,128]{3,2,1,0:T(8,128)(2,1)S(1)}, bf16[4,2,512,128]{3,2,1,0:T(8,128)(2,1)S(1)}, u32[]{:S(2)}, u32[]{:S(2)}) collective-permute-start(bf16[4,2,512,128]{3,2,1,0:T(8,128)(2,1)S(1)} %get-tuple-element.62.kv_ref.refs_3_), channel_id=1, source_target_pairs={{0,16},{8,24},{16,0},{24,8},{1,17},{9,25},{17,1},{25,9},{2,18},{10... | collective-permute-start | bytes 3145736 | tf_op jit(solution)/shard_map/ppermute | solution.py:348
  84.8 48.4 %collective-permute-start.17 = (bf16[4,2,512,128]{3,2,1,0:T(8,128)(2,1)S(1)}, bf16[4,2,512,128]{3,2,1,0:T(8,128)(2,1)S(1)}, u32[]{:S(2)}, u32[]{:S(2)}) collective-permute-start(bf16[4,2,512,128]{3,2,1,0:T(8,128)(2,1)S(1)} %get-tuple-element.62.kv_ref.refs_3_), channel_id=1, source_target_pairs={{0,4},{1,5},{2,6},{3,7},{4,0},{5,1},{6,2},{7,3},{8,12},{9,13},{10,... | collective-permute-start | bytes 3145736 | tf_op jit(solution)/shard_map/ppermute | solution.py:348
  106.5 149.8 %collective-permute-start.21 = (bf16[4,2,512,128]{3,2,1,0:T(8,128)(2,1)S(1)}, bf16[4,2,512,128]{3,2,1,0:T(8,128)(2,1)S(1)}, u32[]{:S(2)}, u32[]{:S(2)}) collective-permute-start(bf16[4,2,512,128]{3,2,1,0:T(8,128)(2,1)S(1)} %get-tuple-element.70.kv_ref.refs_3_), channel_id=1, source_target_pairs={{0,8},{8,0},{16,24},{24,16},{1,9},{9,1},{17,25},{25,17},{2,10},{10... | collective-permute-start | bytes 3145736 | tf_op jit(solution)/shard_map/ppermute | solution.py:348
  107.7 150.0 %collective-permute-start.22 = (bf16[4,2,512,128]{3,2,1,0:T(8,128)(2,1)S(1)}, bf16[4,2,512,128]{3,2,1,0:T(8,128)(2,1)S(1)}, u32[]{:S(2)}, u32[]{:S(2)}) collective-permute-start(bf16[4,2,512,128]{3,2,1,0:T(8,128)(2,1)S(1)} %get-tuple-element.70.kv_ref.refs_3_), channel_id=1, source_target_pairs={{0,16},{8,24},{16,0},{24,8},{1,17},{9,25},{17,1},{25,9},{2,18},{10... | collective-permute-start | bytes 3145736 | tf_op jit(solution)/shard_map/ppermute | solution.py:348
  133.2 124.7 %collective-permute-start.23 = (bf16[4,2,512,128]{3,2,1,0:T(8,128)(2,1)S(1)}, bf16[4,2,512,128]{3,2,1,0:T(8,128)(2,1)S(1)}, u32[]{:S(2)}, u32[]{:S(2)}) collective-permute-start(bf16[4,2,512,128]{3,2,1,0:T(8,128)(2,1)S(1)} %get-tuple-element.70.kv_ref.refs_3_), channel_id=1, source_target_pairs={{0,4},{1,5},{2,6},{3,7},{4,0},{5,1},{6,2},{7,3},{8,12},{9,13},{10,... | collective-permute-start | bytes 3145736 | tf_op jit(solution)/shard_map/ppermute | solution.py:348
  256.3 126.4 %copy-start.10 = (bf16[2048,128]{1,0:T(8,128)(2,1)}, bf16[2048,128]{1,0:T(8,128)(2,1)S(1)}, u32[]{:S(2)}) copy-start(bf16[2048,128]{1,0:T(8,128)(2,1)S(1)} %shard_map.28) | copy-start | bytes 1572868
  256.4 333.2 %collective-permute-start.10 = (bf16[1,2,512,128]{3,2,1,0:T(8,128)(2,1)}, bf16[1,2,512,128]{3,2,1,0:T(8,128)(2,1)}, u32[]{:S(2)}, u32[]{:S(2)}) collective-permute-start(bf16[1,2,512,128]{3,2,1,0:T(8,128)(2,1)} %get-tuple-element.55), channel_id=1, source_target_pairs={{0,6},{1,7},{2,4},{3,5},{4,2},{5,3},{6,0},{7,1},{8,14},{9,15},{10,... | collective-permute-start | bytes 786440 | tf_op jit(solution)/shard_map/ppermute | solution.py:348
  257.7 125.9 %collective-permute-start.3 = (bf16[4,2,512,128]{3,2,1,0:T(8,128)(2,1)S(1)}, bf16[4,2,512,128]{3,2,1,0:T(8,128)(2,1)S(1)}, u32[]{:S(2)}, u32[]{:S(2)}) collective-permute-start(bf16[4,2,512,128]{3,2,1,0:T(8,128)(2,1)S(1)} %get-tuple-element.46.kv_ref.refs_1_), channel_id=1, source_target_pairs={{0,8},{8,0},{16,24},{24,16},{1,9},{9,1},{17,25},{25,17},{2,10},{10... | collective-permute-start | bytes 3145736 | tf_op jit(solution)/shard_map/ppermute | solution.py:348
  258.0 127.1 %collective-permute-start.4 = (bf16[4,2,512,128]{3,2,1,0:T(8,128)(2,1)S(1)}, bf16[4,2,512,128]{3,2,1,0:T(8,128)(2,1)S(1)}, u32[]{:S(2)}, u32[]{:S(2)}) collective-permute-start(bf16[4,2,512,128]{3,2,1,0:T(8,128)(2,1)S(1)} %get-tuple-element.46.kv_ref.refs_1_), channel_id=1, source_target_pairs={{0,16},{8,24},{16,0},{24,8},{1,17},{9,25},{17,1},{25,9},{2,18},{10... | collective-permute-start | bytes 3145736 | tf_op jit(solution)/shard_map/ppermute | solution.py:348
  382.7 0.8 copy-start.12
  383.6 48.5 %collective-permute-start.5 = (bf16[4,2,512,128]{3,2,1,0:T(8,128)(2,1)S(1)}, bf16[4,2,512,128]{3,2,1,0:T(8,128)(2,1)}, u32[]{:S(2)}, u32[]{:S(2)}) collective-permute-start(bf16[4,2,512,128]{3,2,1,0:T(8,128)(2,1)S(1)} %get-tuple-element.46.kv_ref.refs_1_), channel_id=1, source_target_pairs={{0,4},{1,5},{2,6},{3,7},{4,0},{5,1},{6,2},{7,3},{8,12},{9,13},{10,... | collective-permute-start | bytes 3145736 | tf_op jit(solution)/shard_map/ppermute | solution.py:348
  403.1 1.0 copy-start.2
  404.1 1.0 copy-start.4
  405.1 1.1 copy-start.16
  406.2 166.0 %copy-start.9 = (bf16[1,2,512,128]{3,2,1,0:T(8,128)(2,1)S(1)}, bf16[1,2,512,128]{3,2,1,0:T(8,128)(2,1)}, u32[]{:S(2)}) copy-start(bf16[1,2,512,128]{3,2,1,0:T(8,128)(2,1)} %copy-done.8) | copy-start | bytes 786436
  406.2 168.7 %all-to-all-start.1 = ((bf16[4,1,512,128]{3,2,1,0:T(8,128)(2,1)}), bf16[4,1,512,128]{3,2,1,0:T(8,128)(2,1)S(1)}, u32[]{:S(2)}, u32[]{:S(2)}) async-start(bf16[4,1,512,128]{3,2,1,0:T(8,128)(2,1)} %get-tuple-element.49), calls=%async_computation.1 | async-start | bytes 1048576 | tf_op jit(solution)/shard_map/all_to_all | solution.py:363
  411.9 177.7 %collective-permute-start.6 = (bf16[4,2,512,128]{3,2,1,0:T(8,128)(2,1)S(1)}, bf16[4,2,512,128]{3,2,1,0:T(8,128)(2,1)}, u32[]{:S(2)}, u32[]{:S(2)}) collective-permute-start(bf16[4,2,512,128]{3,2,1,0:T(8,128)(2,1)S(1)} %all-to-all-done.2.kv_ref.refs_6_), channel_id=1, source_target_pairs={{0,8},{8,0},{16,24},{24,16},{1,9},{9,1},{17,25},{25,17},{2,10},{10... | collective-permute-start | bytes 3145736 | tf_op jit(solution)/shard_map/ppermute | solution.py:348
  432.1 157.5 %collective-permute-start.7 = (bf16[4,2,512,128]{3,2,1,0:T(8,128)(2,1)S(1)}, bf16[4,2,512,128]{3,2,1,0:T(8,128)(2,1)}, u32[]{:S(2)}, u32[]{:S(2)}) collective-permute-start(bf16[4,2,512,128]{3,2,1,0:T(8,128)(2,1)S(1)} %all-to-all-done.2.kv_ref.refs_6_), channel_id=1, source_target_pairs={{0,16},{8,24},{16,0},{24,8},{1,17},{9,25},{17,1},{25,9},{2,18},{10... | collective-permute-start | bytes 3145736 | tf_op jit(solution)/shard_map/ppermute | solution.py:348
  432.1 1.2 copy-start.3
  433.3 1.2 copy-start.5
  434.5 1.3 copy-start.17
  435.9 1.2 copy-start.19
  572.2 17.3 %collective-permute-start.11 = (bf16[1,2,512,128]{3,2,1,0:T(8,128)(2,1)S(1)}, bf16[1,2,512,128]{3,2,1,0:T(8,128)(2,1)S(1)}, u32[]{:S(2)}, u32[]{:S(2)}) collective-permute-start(bf16[1,2,512,128]{3,2,1,0:T(8,128)(2,1)S(1)} %copy-done.9), channel_id=1, source_target_pairs={{0,7},{1,6},{2,5},{3,4},{4,3},{5,2},{6,1},{7,0},{8,15},{9,14},{10,... | collective-permute-start | bytes 786440 | tf_op jit(solution)/shard_map/ppermute | solution.py:348
  574.9 242.9 %all-to-all-start = ((bf16[4,512,128]{2,1,0:T(8,128)(2,1)}), bf16[4,512,128]{2,1,0:T(8,128)(2,1)S(1)}, u32[]{:S(2)}, u32[]{:S(2)}) async-start(bf16[4,512,128]{2,1,0:T(8,128)(2,1)} %bitcast.2), calls=%async_computation | async-start | bytes 1048576 | tf_op jit(solution)/shard_map/all_to_all | solution.py:363
  589.6 201.5 %copy-start.11 = (bf16[2048,128]{1,0:T(8,128)(2,1)S(1)}, bf16[2048,128]{1,0:T(8,128)(2,1)}, u32[]{:S(2)}) copy-start(bf16[2048,128]{1,0:T(8,128)(2,1)} %copy-done.10) | copy-start | bytes 1572868
  589.6 201.5 %copy-start.13 = (bf16[2048,128]{1,0:T(8,128)(2,1)S(1)}, bf16[2048,128]{1,0:T(8,128)(2,1)}, u32[]{:S(2)}) copy-start(bf16[2048,128]{1,0:T(8,128)(2,1)} %copy-done.12) | copy-start | bytes 1572868
  795.2 2.2 collective-permute-start.24
  795.3 10.3 %collective-permute-start.25 = (bf16[3,512,128]{2,1,0:T(8,128)(2,1)S(1)}, bf16[3,512,128]{2,1,0:T(8,128)(2,1)S(1)}, u32[]{:S(2)}, u32[]{:S(2)}) collective-permute-start(bf16[3,512,128]{2,1,0:T(8,128)(2,1)S(1)} %get-tuple-element.75), channel_id=1, source_target_pairs={{0,2},{1,3},{2,0},{3,1},{4,6},{5,7},{6,4},{7,5},{8,10},{9,11},{10,... | collective-permute-start | bytes 1179656 | tf_op jit(solution)/shard_map/ppermute | solution.py:348
  796.0 18.6 %collective-permute-start.26 = (bf16[3,512,128]{2,1,0:T(8,128)(2,1)S(1)}, bf16[3,512,128]{2,1,0:T(8,128)(2,1)S(1)}, u32[]{:S(2)}, u32[]{:S(2)}) collective-permute-start(bf16[3,512,128]{2,1,0:T(8,128)(2,1)S(1)} %get-tuple-element.76), channel_id=1, source_target_pairs={{0,3},{1,2},{2,1},{3,0},{4,7},{5,6},{6,5},{7,4},{8,11},{9,10},{10,... | collective-permute-start | bytes 1179656 | tf_op jit(solution)/shard_map/ppermute | solution.py:348
  (2 other events, 1.5 us)

commit v2 on v1

--- a/solution.py
+++ b/solution.py
@@ -12,18 +12,19 @@
 BLOCK = 2048
 HEAD_ROWS = 80
 LIMIT = 1e30
+UNIT = 2e9
 F32 = jnp.float32
 BF16 = jnp.bfloat16
 NT = (((1,), (1,)), ((), ()))
 ANY = pl.BlockSpec(memory_space=pl.ANY)
 
 
-def params(mib=40):
+def params(mib=58):
     return pltpu.CompilerParams(vmem_limit_bytes=mib << 20)
 
 
 def cost(units):
-    return pl.CostEstimate(flops=int(units * 1e10), bytes_accessed=1 << 20, transcendentals=0)
+    return pl.CostEstimate(flops=int(units * UNIT), bytes_accessed=1 << 20, transcendentals=0)
 
 
 def staged(moves, buf_ref, in_sem, out_sem):
@@ -83,62 +84,44 @@
     return move(kernel, rank, [qkv], shapes, n, rows, 0.2)
 
 
-def merge(rank, pieces):
-    rows, n = pieces[0].shape[2], len(pieces)
-
-    def kernel(me, ins, outs):
-        q, kv = outs
-        moves = [(ins[k].at[0, 1 + i], kv.at[k, i]) for k in range(n) for i in range(2)]
-        return moves + [(ins[k].at[0, 0], q.at[jnp.bitwise_xor(me, k)]) for k in range(n)]
-
-    shapes = [(n, rows, LANES), (n, 2, rows, LANES)]
-    shapes = [jax.ShapeDtypeStruct(shape, BF16) for shape in shapes]
-    return move(kernel, rank, pieces, shapes, 3 * n, rows, 0.2)
-
-
-def regroup(rank, arrays):
-    groups, rows, _ = arrays[0].shape
-    n = len(arrays)
-
-    def kernel(me, ins, outs):
-        return [
-            (ins[p].at[jnp.bitwise_xor(me, k)], out.at[p])
-            for k, out in enumerate(outs)
-            for p in range(n)
-        ]
-
-    shapes = [jax.ShapeDtypeStruct((n, rows, LANES), BF16)] * groups
-    return move(kernel, rank, arrays, shapes, n * groups, rows, 0.2)
-
-
-def place_early(rank, pieces, shape):
-    n, rows, _ = pieces[0].shape
-    width = shape[1] // len(pieces)
+def pack_last(rank, qkv, far, first):
+    groups, _, rows, _ = far.shape
+    width = qkv.shape[1] // 3
 
     def kernel(me, ins, outs):
         moves = []
-        for k, piece in enumerate(ins):
-            for p in range(n):
-                start = pl.multiple_of(jnp.bitwise_xor(me, k) * width + p * LANES, LANES)
-                moves.append((piece.at[p], outs[0].at[:, pl.ds(start, LANES)]))
+        for k, out in enumerate(outs):
+            owner = jnp.bitwise_xor(me, k)
+            start = pl.multiple_of(owner * (width // groups) + first * LANES, LANES)
+            for n in range(3):
+                moves.append((ins[0].at[:, pl.ds(n * width + start, LANES)], out.at[0, n]))
+            for n in range(2):
+                moves.append((ins[1].at[owner, n], out.at[0, 3 + n]))
         return moves
 
+    shapes = [jax.ShapeDtypeStruct((1, 5, rows, LANES), BF16)] * groups
+    return move(kernel, rank, [qkv, far], shapes, 5 * groups, rows, 0.2)
+
+
+def place(rank, pieces, pairs, base, shape):
+    rows, _ = pieces[0][0].shape
+    groups = len(pieces[0])
+    width = shape[1] // groups
+    flat = [piece for pair in pieces for piece in pair]
+    n = len(flat)
+
+    def kernel(me, ins, outs):
+        moves = []
+        for m, piece in enumerate(ins[:n]):
+            owner = jnp.bitwise_xor(me, m % groups)
+            start = pl.multiple_of(owner * width + pairs[m // groups] * LANES, LANES)
+            moves.append((piece, outs[0].at[:, pl.ds(start, LANES)]))
+        return moves
+
     out = jax.ShapeDtypeStruct(shape, BF16)
-    return move(kernel, rank, pieces, out, n * len(pieces), rows, 0.2)
-
-
-def place_last(rank, pieces, base, pair):
-    groups, rows, _ = pieces.shape
-    width = base.shape[1] // groups
-
-    def kernel(me, ins, outs):
-        return [
-            (ins[0].at[k], outs[0].at[:, pl.ds(k * width + pair * LANES, LANES)])
-            for k in range(groups)
-        ]
-
-    out = jax.ShapeDtypeStruct(base.shape, BF16)
-    return move(kernel, rank, [pieces, base], out, groups, rows, 0.1, {2: 0})
+    if base is None:
+        return move(kernel, rank, flat, out, n, rows, 0.2)
+    return move(kernel, rank, flat + [base], out, n, rows, 0.2, {n + 1: 0})
 
 
 def prepare(kv_refs, keys_ref, values_ref):
@@ -165,14 +148,20 @@
     return jnp.dot(values, probs, preferred_element_type=F32)
 
 
-def first_kernel(q_ref, kv_ref, qe_ref, acc_ref, keys_ref, values_ref):
-    h = pl.program_id(1)
-
-    @pl.when((pl.program_id(0) == 0) & (h == 0))
+def first_kernel(rank_ref, *refs, n, kinds):
+    pieces, outs = refs[:n], refs[n:]
+    joined, (qe_ref, acc_ref, query_ref, keys_ref, values_ref) = outs[: kinds // 2], outs[kinds // 2 :]
+    i, h = pl.program_id(0), pl.program_id(1)
+
+    @pl.when((i == 0) & (h == 0))
     def _():
-        prepare([kv_ref], keys_ref, values_ref)
-
-    query = q_ref[...] * jnp.asarray(HEAD_DIM**-0.5, BF16)
+        for k, piece in enumerate(pieces):
+            query_ref[jnp.bitwise_xor(rank_ref[0], k)] = piece[0, 0]
+            for m, out in enumerate(joined):
+                out[k] = piece[0, 1 + 2 * m : 3 + 2 * m]
+        prepare(joined[:1], keys_ref, values_ref)
+
+    query = query_ref[i] * jnp.asarray(HEAD_DIM**-0.5, BF16)
     lane = lax.broadcasted_iota(jnp.int32, query.shape, 1)
     mine = (lane // HEAD_DIM) == h
     query = jnp.where(mine, query, jnp.zeros_like(query))
@@ -184,31 +173,34 @@
     acc_ref[0] = weigh(keys_ref[0, h], values_ref[0, h], query)
 
 
-def first(q, kv):
-    tokens = q.shape[0] * q.shape[1]
-    tile = min(512, tokens)
-    return pl.pallas_call(
-        first_kernel,
-        grid=(tokens // tile, 2),
-        in_specs=[
-            pl.BlockSpec((tile, LANES), lambda i, h: (i, 0)),
-            pl.BlockSpec(kv.shape, lambda i, h: (0, 0, 0, 0)),
+def first(rank, pieces):
+    _, kinds, rows, _ = pieces[0].shape
+    n = len(pieces)
+    tokens = n * rows
+    whole = (n, 2, rows, LANES)
+    many = kinds // 2
+    qe, acc = (2, tokens, LANES), (2, HEAD_ROWS, tokens)
+    *kvs, qe, acc = pl.pallas_call(
+        functools.partial(first_kernel, n=n, kinds=kinds),
+        grid=(n, 2),
+        in_specs=[pl.BlockSpec(memory_space=pltpu.SMEM)]
+        + [pl.BlockSpec(pieces[0].shape, lambda i, h: (0, 0, 0, 0))] * n,
+        out_specs=[pl.BlockSpec(whole, lambda i, h: (0, 0, 0, 0))] * many
+        + [
+            pl.BlockSpec((1, rows, LANES), lambda i, h: (h, i, 0)),
+            pl.BlockSpec((1, HEAD_ROWS, rows), lambda i, h: (h, 0, i)),
         ],
-        out_specs=[
-            pl.BlockSpec((1, tile, LANES), lambda i, h: (h, i, 0)),
-            pl.BlockSpec((1, HEAD_ROWS, tile), lambda i, h: (h, 0, i)),
-        ],
-        out_shape=[
-            jax.ShapeDtypeStruct((2, tokens, LANES), BF16),
-            jax.ShapeDtypeStruct((2, HEAD_ROWS, tokens), F32),
-        ],
+        out_shape=[jax.ShapeDtypeStruct(whole, BF16)] * many
+        + [jax.ShapeDtypeStruct(qe, BF16), jax.ShapeDtypeStruct(acc, F32)],
         scratch_shapes=[
+            pltpu.VMEM((n, rows, LANES), BF16),
             pltpu.VMEM((1, 2, tokens, LANES), BF16),
             pltpu.VMEM((1, 2, HEAD_ROWS, tokens), BF16),
         ],
         compiler_params=params(),
         cost_estimate=cost(1),
-    )(q.reshape(tokens, LANES), kv)
+    )(rank, *pieces)
+    return kvs, (qe, acc)
 
 
 def blocks_of(kvs, tokens):
@@ -236,7 +228,7 @@
 def more(qe, acc, kvs):
     tokens = qe.shape[1]
     n = blocks_of(kvs, tokens)
-    tile = min(512, tokens)
+    tile = kvs[0].shape[2]
     state = pl.BlockSpec((1, HEAD_ROWS, tile), lambda i, h: (h, 0, i))
     return pl.pallas_call(
         functools.partial(more_kernel, n_refs=len(kvs), n=n),
@@ -255,9 +247,9 @@
     )(qe, acc, *kvs)
 
 
-def last_kernel(qe_ref, acc_ref, *refs, n_refs, n_all, n):
+def last_kernel(rank_ref, qe_ref, acc_ref, *refs, n_refs, n_all, n):
     kv_refs, all_refs = refs[:n_refs], refs[n_refs : n_refs + n_all]
-    out_ref, keys_ref, values_ref, sum_ref, both_ref, buf_ref, sem = refs[n_refs + n_all :]
+    *out_refs, keys_ref, values_ref, sum_ref, both_ref, buf_ref, sem = refs[n_refs + n_all :]
     h = pl.program_id(1)
 
     @pl.when((pl.program_id(0) == 0) & (h == 0))
@@ -309,43 +301,61 @@
     @pl.when(h == 1)
     def _():
         joined = jnp.concatenate([both_ref[0], both_ref[1]], axis=0)
-        out_ref[...] = joined.T.astype(BF16)
-
-
-def last(qe, acc, kvs, all_kvs):
+        joined = joined.T.astype(BF16)
+        for k, out_ref in enumerate(out_refs):
+
+            @pl.when(pl.program_id(0) == jnp.bitwise_xor(rank_ref[0], k))
+            def _(out_ref=out_ref):
+                out_ref[...] = joined
+
+
+def last(rank, qe, acc, kvs, all_kvs):
     n_all = len(all_kvs)
     tokens = qe.shape[1]
     n = blocks_of(kvs, tokens)
-    tile = min(512, tokens)
     rows = kvs[0].shape[2]
-    out = pl.pallas_call(
+    groups = tokens // rows
+    return pl.pallas_call(
         functools.partial(last_kernel, n_refs=len(kvs), n_all=n_all, n=n),
-        grid=(tokens // tile, 2),
+        grid=(groups, 2),
         in_specs=[
-            pl.BlockSpec((1, tile, LANES), lambda i, h: (h, i, 0)),
-            pl.BlockSpec((1, HEAD_ROWS, tile), lambda i, h: (h, 0, i)),
+            pl.BlockSpec(memory_space=pltpu.SMEM),
+            pl.BlockSpec((1, rows, LANES), lambda i, h: (h, i, 0)),
+            pl.BlockSpec((1, HEAD_ROWS, rows), lambda i, h: (h, 0, i)),
         ]
         + [pl.BlockSpec(kv.shape, lambda i, h: (0, 0, 0, 0)) for kv in kvs]
         + [ANY] * n_all,
-        out_specs=pl.BlockSpec((tile, LANES), lambda i, h: (i, 0)),
-        out_shape=jax.ShapeDtypeStruct((tokens, LANES), BF16),
+        out_specs=[pl.BlockSpec((rows, LANES), lambda i, h: (0, 0))] * groups,
+        out_shape=[jax.ShapeDtypeStruct((rows, LANES), BF16)] * groups,
         scratch_shapes=[
             pltpu.VMEM((n, 2, tokens, LANES), BF16),
             pltpu.VMEM((n, 2, HEAD_ROWS, tokens), BF16),
-            pltpu.VMEM((HEAD_ROWS, tile), F32),
-            pltpu.VMEM((2, HEAD_DIM, tile), F32),
+            pltpu.VMEM((HEAD_ROWS, rows), F32),
+            pltpu.VMEM((2, HEAD_DIM, rows), F32),
             pltpu.VMEM((2, rows, LANES), BF16),
             pltpu.SemaphoreType.DMA,
         ],
         compiler_params=params(),
         cost_estimate=cost(n),
-    )(qe, acc, *kvs, *all_kvs)
-    return out.reshape(tokens // rows, rows, LANES)
+    )(rank, qe, acc, *kvs, *all_kvs)
 
 
 def swap(x, axis, bit):
     size = lax.axis_size(axis)
     return lax.ppermute(x, axis, [(i, i ^ bit) for i in range(size)])
+
+
+class Chain:
+    def __init__(self):
+        self.token = None
+
+    def __call__(self, step, arrays, *rest):
+        leaves, tree = jax.tree.flatten(arrays)
+        if self.token is not None:
+            self.token, *leaves = lax.optimization_barrier((self.token, *leaves))
+        out = step(*jax.tree.unflatten(tree, leaves), *rest)
+        self.token = jax.tree.leaves(out)[0]
+        return out
 
 
 def on_device(qkv):
@@ -356,43 +366,79 @@
     pairs = width // groups // LANES
     bits = lax.axis_size("blk").bit_length() - 1
     rank = jnp.bitwise_and(lax.axis_index("head"), groups - 1).astype(jnp.int32).reshape(1)
-    teams = [list(range(groups)), list(range(groups, size))]
     ranks = tuple(range(groups))
-
-    def exchange(x):
-        return lax.all_to_all(
-            x, "head", split_axis=0, concat_axis=0, tiled=True, axis_index_groups=teams
-        )
-
-    order = [((1, 2), ranks), ((0,), ranks)] + [((1, 2), ((k,),)) for k in range(groups)]
-    kv_all, q_all, *direct = pack(rank, qkv, 0, groups, order)
-    far = [[swap(direct[k], "head", groups ^ k) for k in range(groups)]]
-    own = [exchange(kv_all)]
-    query = [exchange(q_all)[:, 0]]
-    near = [[swap(own[0], "blk", 1 << bit) for bit in range(bits)]]
-    for p in range(1, pairs):
-        pieces = pack(rank, qkv, p, groups, [((0, 1, 2), ((k,),)) for k in range(groups)])
-        pieces = [pieces[0]] + [swap(pieces[k], "head", k) for k in range(1, groups)]
-        q, kv = merge(rank, pieces)
-        query.append(q)
-        own.append(kv)
-        far.append([swap(kv, "head", groups)])
-        near.append([swap(kv, "blk", 1 << bit) for bit in range(bits)])
-
-    states = [first(query[p], own[p]) for p in range(pairs)]
-    outs = []
-    for p in range(pairs):
-        qe, acc = states[p]
-        everything = [own[p]] + near[p] + far[p]
-        if p < pairs - 1:
-            outs.append(last(qe, acc, near[p] + far[p], everything))
-        else:
-            acc = more(qe, acc, near[p])
-            outs.append(last(qe, acc, far[p], everything))
-    early = regroup(rank, outs[:-1])
-    early = [early[0]] + [swap(early[k], "head", k) for k in range(1, groups)]
-    result = place_early(rank, early, (rows, width))
-    return place_last(rank, exchange(outs[-1]), result, pairs - 1)
+    chain = Chain()
+
+    def spread(pieces, after=None):
+        if after is not None:
+            _, pieces = lax.optimization_barrier((after, pieces))
+        return [pieces[0]] + [swap(pieces[k], "head", k) for k in range(1, groups)]
+
+    def nearby(kv):
+        return [swap(kv, "blk", 1 << bit) for bit in range(bits)]
+
+    def fetch(p):
+        if p < end:
+            return chain(lambda r, x: pack(r, x, p, groups, each), (rank, qkv))
+        return chain(lambda r, x, y: pack_last(r, x, y, end), (rank, qkv, raw))
+
+    each = [((0, 1, 2), ((k,),)) for k in ranks]
+    end = pairs - 1
+    late = max(end - 1, 0)
+    packed, pieces, own, near, far, state, returned = {}, {}, {}, {}, {}, {}, {}
+
+    def open_(p):
+        kvs, state[p] = chain(first, (rank, pieces[p]))
+        own[p] = kvs[0]
+        near[p] = nearby(own[p])
+        if p == end:
+            far[p] = kvs[1:]
+
+    def cross(p):
+        kv = own[p]
+        before = raw if p == 0 else far[p - 1]
+        _, _, kv = lax.optimization_barrier((before, chain.token, kv))
+        far[p] = [swap(kv, "head", groups)]
+
+    def grow(p):
+        qe, acc = state[p]
+        state[p] = qe, chain(more, (qe, acc, near[p]))
+
+    def close(p, new):
+        qe, acc = state[p]
+        returned[p] = spread(chain(last, (rank, qe, acc, new, [own[p]] + near[p] + far[p])))
+
+    (raw,) = chain(lambda r, x: pack(r, x, end, groups, [((1, 2), ranks)]), (rank, qkv))
+    packed[0] = fetch(0)
+    pieces[0] = spread(packed[0])
+    for p in range(1, end):
+        packed[p] = fetch(p)
+    if end > 1:
+        pieces[1] = spread(packed[1], pieces[0])
+    _, raw = lax.optimization_barrier((pieces[min(1, late)], raw))
+    raw = swap(raw, "head", groups)
+    for p in range(end):
+        open_(p)
+        if p + 2 < end:
+            pieces[p + 2] = spread(packed[p + 2], (pieces[p + 1], chain.token))
+        cross(p)
+        if p == late:
+            pieces[end] = spread(fetch(end))
+        if p > 0:
+            grow(p - 1)
+    grow(late)
+    open_(end)
+    if late > 0:
+        close(0, far[0])
+    close(end, near[end] + far[end])
+    for p in range(1, end):
+        close(p, far[p])
+    if late == 0:
+        close(0, far[0])
+    early = [p for p in range(pairs) if p != late]
+    shape = (rows, width)
+    result = chain(lambda r, x: place(r, x, early, None, shape), (rank, [returned[p] for p in early]))
+    return chain(lambda r, x, y: place(r, x, [late], y, shape), (rank, [returned[late]], result))
 
 
 def solution(mesh):

time: 824 us -> 1140 us (1.38)
  Pallas kernels: 675 us -> 1030 us
  waiting for transfers between devices: 85.1 us -> 57.7 us
  local copies, waits for them, and re-layouts: 17.7 us -> 4.15 us
    pallas_call x4, Pallas kernels: 583 us -> 893 us  [last(): pl.pallas_call(functools.partial(last_kernel, n_refs=len(kvs), n_all=n_al...]
    pallas_call x1 -> x3, Pallas kernels: 18 us -> 61.1 us  [more(): pl.pallas_call(functools.partial(more_kernel, n_refs=len(kvs), n=n), grid...]
    ppermute x27 -> x36, waiting for transfers between devices: 85.1 us -> 57.7 us  [swap(): return lax.ppermute(x, axis, [(i, i ^ bit) for i in range(size)])]
    unnamed x40 -> x82, local copies, waits for them, and re-layouts: 17.7 us -> 4.15 us
    all_to_all x3 -> x0, starting transfers between devices: 13.1 us -> none  [exchange(): lax.all_to_all(x, 'head', split_axis=0, concat_axis=0, tiled=True, axis_i...]
    ppermute x27 -> x36, starting transfers between devices: 27.6 us -> 39.5 us  [swap(): return lax.ppermute(x, axis, [(i, i ^ bit) for i in range(size)])]
    pallas_call x10 -> x7, Pallas kernels: 29.9 us -> 18.1 us  [move(): pl.pallas_call(body, in_specs=[pl.BlockSpec(memory_space=pltpu.SMEM)] + [...]
  transfers between devices with their start and end apart: 30 -> 36, of which waited for: 8 -> 10; matrix products, arithmetic and copies ran while one was open for 0% -> 0% of each run, Pallas kernels for 82% -> 89%
where the time goes in v2:
time: 1140 us; the launch traced here: 1130 us
  Pallas kernels  1030 us (90%)
  waiting for transfers between devices  57.7 us (5%)
  starting transfers between devices  39.5 us (3%)
    pallas_call x4, Pallas kernels, last(): pl.pallas_call(functools.partial(last_kernel, n_refs=len(kvs), n_all=n_al...  893 us
    pallas_call x3, Pallas kernels, more(): pl.pallas_call(functools.partial(more_kernel, n_refs=len(kvs), n=n), grid...  61.1 us
    ppermute x36, waiting for transfers between devices, swap(): return lax.ppermute(x, axis, [(i, i ^ bit) for i in range(size)])  57.7 us
    pallas_call x4, Pallas kernels, first(): pl.pallas_call(functools.partial(first_kernel, n=n, kinds=kinds), grid=(n...  53.6 us
    ppermute x36, starting transfers between devices, swap(): return lax.ppermute(x, axis, [(i, i ^ bit) for i in range(size)])  39.5 us
  transfers between devices with their start and end apart: 36, of which 10 were waited for; matrix products, arithmetic and copies ran while one was open for 0% of the time, Pallas kernels for 89%

profile of v2, /device:TPU:1, one launch (start us, length us, event | category | flops | bytes accessed | tf_op | source)
XLA Modules:
  0.0 1127.3 jit_solution(16292553249740370843)
XLA Ops:
  0.0 2.3 shard_map.17
  2.3 2.6 shard_map.18
  5.1 2.8 collective-permute-start.1
  7.9 2.7 shard_map.19
  10.5 2.7 shard_map.20
  13.3 4.1 collective-permute-done.1.refs_2_
  17.4 8.4 collective-permute-done.2.refs_3_
  26.6 13.4 %shard_map.21 = (bf16[4,2,512,128]{3,2,1,0:T(8,128)(2,1)}, bf16[2,2048,128]{2,1,0:T(8,128)(2,1)}, f32[2,80,2048]{2,1,0:T(8,128)}) custom-call(s32[1]{0:T(128)} %bitcast.rank_ref, bf16[1,3,512,128]{3,2,1,0:T(8,128)(2,1)} %get-tuple-element.169.refs_0_, bf16[1,3,512,128]{3,2,1,0:T(8,128)(2,1)} %copy-done.36, bf16[1,3,512,128]{3,2,1,0:T(8,128)(2,1)} %copy-done.37, ...), custom_call_target="tpu_custom_call" | custom-call | flops 2000000000 | bytes 1048576 | tf_op jit(solution)/shard_map/pallas_call | solution.py:183
  40.1 1.4 collective-permute-start.6
  41.4 1.2 collective-permute-start.7
  42.7 0.8 collective-permute-start.3
  43.5 1.3 collective-permute-start.4
  45.2 9.0 collective-permute-done.4.refs_2_
  54.2 8.9 collective-permute-done.5.refs_3_
  63.1 1.3 collective-permute-start.9
  64.4 0.8 collective-permute-start.10
  65.2 2.3 collective-permute-start.11
  67.6 13.2 %shard_map.22 = (bf16[4,2,512,128]{3,2,1,0:T(8,128)(2,1)}, bf16[2,2048,128]{2,1,0:T(8,128)(2,1)}, f32[2,80,2048]{2,1,0:T(8,128)}) custom-call(s32[1]{0:T(128)} %bitcast.rank_ref, bf16[1,3,512,128]{3,2,1,0:T(8,128)(2,1)} %get-tuple-element.182.refs_0_, bf16[1,3,512,128]{3,2,1,0:T(8,128)(2,1)} %copy-done.33, bf16[1,3,512,128]{3,2,1,0:T(8,128)(2,1)} %copy-done.34, ...), custom_call_target="tpu_custom_call" | custom-call | flops 2000000000 | bytes 1048576 | tf_op jit(solution)/shard_map/pallas_call | solution.py:183
  80.8 1.1 collective-permute-start.12
  81.9 20.3 %shard_map.23.acc_ref = f32[2,80,2048]{2,1,0:T(8,128)} custom-call(bf16[2,2048,128]{2,1,0:T(8,128)(2,1)} %get-tuple-element.234.qe_ref, f32[2,80,2048]{2,1,0:T(8,128)} %get-tuple-element.190.acc_ref, bf16[4,2,512,128]{3,2,1,0:T(8,128)(2,1)} %copy-done.6, bf16[4,2,512,128]{3,2,1,0:T(8,128)(2,1)} %copy-done.8), custom_call_target="tpu_custom_call", output_to_operand_aliasing={{}: (1, {})} | custom-call | flops 4000000000 | bytes 1048576 | tf_op jit(solution)/shard_map/pallas_call | solution.py:233
  102.2 1.4 collective-permute-start.13
  103.6 13.2 %shard_map.24 = (bf16[4,2,512,128]{3,2,1,0:T(8,128)(2,1)}, bf16[2,2048,128]{2,1,0:T(8,128)(2,1)}, f32[2,80,2048]{2,1,0:T(8,128)}) custom-call(s32[1]{0:T(128)} %bitcast.rank_ref, bf16[1,3,512,128]{3,2,1,0:T(8,128)(2,1)} %get-tuple-element.201.refs_0_, bf16[1,3,512,128]{3,2,1,0:T(8,128)(2,1)} %copy-done.30, ...), custom_call_target="tpu_custom_call" | custom-call | flops 2000000000 | bytes 1048576 | tf_op jit(solution)/shard_map/pallas_call | solution.py:183
  116.8 0.9 collective-permute-start.14
  118.7 3.3 shard_map.25
  122.0 3.5 collective-permute-done.13.refs_1_.refs_3_
  125.5 4.6 collective-permute-start.16
  130.2 1.3 collective-permute-start.17
  131.5 8.6 collective-permute-done.14.refs_0_.refs_2_
  140.1 3.8 collective-permute-start.18
  143.8 20.2 %shard_map.26.acc_ref = f32[2,80,2048]{2,1,0:T(8,128)} custom-call(bf16[2,2048,128]{2,1,0:T(8,128)(2,1)} %get-tuple-element.258.qe_ref, f32[2,80,2048]{2,1,0:T(8,128)} %get-tuple-element.214.acc_ref, bf16[4,2,512,128]{3,2,1,0:T(8,128)(2,1)} %collective-permute-done.12.refs_0_.refs_2_, bf16[4,2,512,128]{3,2,1,0:T(8,128)(2,1)} %copy-done.9), custom_call_target="tpu_custom_call", output_to_operand_aliasing={{}: (1, {})} | custom-call | flops 4000000000 | bytes 1048576 | tf_op jit(solution)/shard_map/pallas_call | solution.py:233
  164.1 1.7 collective-permute-done.19.refs_0_.refs_4_
  165.8 20.6 %shard_map.27.acc_ref = f32[2,80,2048]{2,1,0:T(8,128)} custom-call(bf16[2,2048,128]{2,1,0:T(8,128)(2,1)} %get-tuple-element.268.qe_ref, f32[2,80,2048]{2,1,0:T(8,128)} %get-tuple-element.220.acc_ref, bf16[4,2,512,128]{3,2,1,0:T(8,128)(2,1)} %copy-done.5, bf16[4,2,512,128]{3,2,1,0:T(8,128)(2,1)} %copy-done.7), custom_call_target="tpu_custom_call", output_to_operand_aliasing={{}: (1, {})} | custom-call | flops 4000000000 | bytes 1048576 | tf_op jit(solution)/shard_map/pallas_call | solution.py:233
  187.2 13.6 %shard_map.28 = (bf16[4,2,512,128]{3,2,1,0:T(8,128)(2,1)}, bf16[4,2,512,128]{3,2,1,0:T(8,128)(2,1)}, bf16[2,2048,128]{2,1,0:T(8,128)(2,1)}, f32[2,80,2048]{2,1,0:T(8,128)}) custom-call(s32[1]{0:T(128)} %bitcast.rank_ref, bf16[1,5,512,128]{3,2,1,0:T(8,128)(2,1)} %get-tuple-element.227.refs_0_, bf16[1,5,512,128]{3,2,1,0:T(8,128)(2,1)} %copy-done.25, ...), custom_call_target="tpu_custom_call" | custom-call | flops 2000000000 | bytes 1048576 | tf_op jit(solution)/shard_map/pallas_call | solution.py:183
  201.4 0.8 collective-permute-start.21
  202.2 10.4 collective-permute-done.22.refs_0_.refs_4_
  212.6 218.8 %shard_map.29 = (bf16[512,128]{1,0:T(8,128)(2,1)}, bf16[512,128]{1,0:T(8,128)(2,1)}, bf16[512,128]{1,0:T(8,128)(2,1)}, bf16[512,128]{1,0:T(8,128)(2,1)}) custom-call(s32[1]{0:T(128)} %bitcast.rank_ref, bf16[2,2048,128]{2,1,0:T(8,128)(2,1)} %get-tuple-element.234.qe_ref, f32[2,80,2048]{2,1,0:T(8,128)} %shard_map.23.acc_ref, ...), custom_call_target="tpu_custom_call" | custom-call | flops 2000000000 | bytes 1048576 | tf_op jit(solution)/shard_map/pallas_call | solution.py:318
  431.4 2.4 collective-permute-start.27
  433.9 2.4 collective-permute-start.28
  436.3 0.9 copy-done.23
  437.7 237.1 %shard_map.30 = (bf16[512,128]{1,0:T(8,128)(2,1)}, bf16[512,128]{1,0:T(8,128)(2,1)}, bf16[512,128]{1,0:T(8,128)(2,1)}, bf16[512,128]{1,0:T(8,128)(2,1)}) custom-call(s32[1]{0:T(128)} %bitcast.rank_ref, bf16[2,2048,128]{2,1,0:T(8,128)(2,1)} %get-tuple-element.246.qe_ref, f32[2,80,2048]{2,1,0:T(8,128)} %get-tuple-element.247.acc_ref, ...), custom_call_target="tpu_custom_call" | custom-call | flops 6000000000 | bytes 1048576 | tf_op jit(solution)/shard_map/pallas_call | solution.py:318
  675.1 218.4 %shard_map.31 = (bf16[512,128]{1,0:T(8,128)(2,1)}, bf16[512,128]{1,0:T(8,128)(2,1)}, bf16[512,128]{1,0:T(8,128)(2,1)}, bf16[512,128]{1,0:T(8,128)(2,1)}) custom-call(s32[1]{0:T(128)} %bitcast.rank_ref, bf16[2,2048,128]{2,1,0:T(8,128)(2,1)} %get-tuple-element.258.qe_ref, f32[2,80,2048]{2,1,0:T(8,128)} %shard_map.26.acc_ref, ...), custom_call_target="tpu_custom_call" | custom-call | flops 2000000000 | bytes 1048576 | tf_op jit(solution)/shard_map/pallas_call | solution.py:318
  893.6 1.2 collective-permute-start.34
  895.7 1.3 collective-permute-start.31
  897.7 218.4 %shard_map.32 = (bf16[512,128]{1,0:T(8,128)(2,1)}, bf16[512,128]{1,0:T(8,128)(2,1)}, bf16[512,128]{1,0:T(8,128)(2,1)}, bf16[512,128]{1,0:T(8,128)(2,1)}) custom-call(s32[1]{0:T(128)} %bitcast.rank_ref, bf16[2,2048,128]{2,1,0:T(8,128)(2,1)} %get-tuple-element.268.qe_ref, f32[2,80,2048]{2,1,0:T(8,128)} %shard_map.27.acc_ref, bf16[4,2,512,128]{3,2,1,0:T(8,128)(2,1)} %copy-done, ...), custom_call_target="tpu_custom_call" | custom-call | flops 2000000000 | bytes 1048576 | tf_op jit(solution)/shard_map/pallas_call | solution.py:318
  1116.4 1.4 collective-permute-start.25
  1119.2 2.6 shard_map.33.refs_4_
  1121.8 2.9 collective-permute-done.26.refs_3_
  1125.3 1.9 shard_map.34
  (124 shorter events, 8.4 us)
Async XLA Ops:
  4.9 8.3 collective-permute-start
  5.1 12.4 %collective-permute-start.1 = (bf16[1,3,512,128]{3,2,1,0:T(8,128)(2,1)}, bf16[1,3,512,128]{3,2,1,0:T(8,128)(2,1)S(1)}, u32[]{:S(2)}, u32[]{:S(2)}) collective-permute-start(bf16[1,3,512,128]{3,2,1,0:T(8,128)(2,1)} %get-tuple-element.166), channel_id=1, source_target_pairs={{0,2},{1,3},{2,0},{3,1},{4,6},{5,7},{6,4},{7,5},{8,10},{9,11},{10,... | collective-permute-start | bytes 1179656 | tf_op jit(solution)/shard_map/ppermute | solution.py:345
  7.8 18.0 %collective-permute-start.2 = (bf16[1,3,512,128]{3,2,1,0:T(8,128)(2,1)}, bf16[1,3,512,128]{3,2,1,0:T(8,128)(2,1)S(1)}, u32[]{:S(2)}, u32[]{:S(2)}) collective-permute-start(bf16[1,3,512,128]{3,2,1,0:T(8,128)(2,1)} %get-tuple-element.167), channel_id=1, source_target_pairs={{0,3},{1,2},{2,1},{3,0},{4,7},{5,6},{6,5},{7,4},{8,11},{9,10},{10,... | collective-permute-start | bytes 1179656 | tf_op jit(solution)/shard_map/ppermute | solution.py:345
  26.6 36.5 %copy-start.28 = (bf16[1,3,512,128]{3,2,1,0:T(8,128)(2,1)S(1)}, bf16[1,3,512,128]{3,2,1,0:T(8,128)(2,1)}, u32[]{:S(2)}) copy-start(bf16[1,3,512,128]{3,2,1,0:T(8,128)(2,1)} %get-tuple-element.197) | copy-start | bytes 1179652
  26.6 36.5 %copy-start.27 = (bf16[1,3,512,128]{3,2,1,0:T(8,128)(2,1)S(1)}, bf16[1,3,512,128]{3,2,1,0:T(8,128)(2,1)}, u32[]{:S(2)}) copy-start(bf16[1,3,512,128]{3,2,1,0:T(8,128)(2,1)} %get-tuple-element.198) | copy-start | bytes 1179652
  26.6 37.8 %copy-start.26 = (bf16[1,3,512,128]{3,2,1,0:T(8,128)(2,1)S(1)}, bf16[1,3,512,128]{3,2,1,0:T(8,128)(2,1)}, u32[]{:S(2)}) copy-start(bf16[1,3,512,128]{3,2,1,0:T(8,128)(2,1)} %get-tuple-element.199) | copy-start | bytes 1179652
  26.6 38.6 %copy-start.10 = (bf16[4,2,512,128]{3,2,1,0:T(8,128)(2,1)S(1)}, bf16[4,2,512,128]{3,2,1,0:T(8,128)(2,1)}, u32[]{:S(2)}) copy-start(bf16[4,2,512,128]{3,2,1,0:T(8,128)(2,1)} %shard_map.17) | copy-start | bytes 3145732
  40.1 25.1 %collective-permute-start.6 = (bf16[4,2,512,128]{3,2,1,0:T(8,128)(2,1)}, bf16[4,2,512,128]{3,2,1,0:T(8,128)(2,1)S(1)}, u32[]{:S(2)}, u32[]{:S(2)}) collective-permute-start(bf16[4,2,512,128]{3,2,1,0:T(8,128)(2,1)} %get-tuple-element.237.refs_1_), channel_id=1, source_target_pairs={{0,8},{8,0},{16,24},{24,16},{1,9},{9,1},{17,25},{25,17},{2,10},{10... | collective-permute-start | bytes 3145736 | tf_op jit(solution)/shard_map/ppermute | solution.py:345
  41.4 39.4 %collective-permute-start.7 = (bf16[4,2,512,128]{3,2,1,0:T(8,128)(2,1)}, bf16[4,2,512,128]{3,2,1,0:T(8,128)(2,1)S(1)}, u32[]{:S(2)}, u32[]{:S(2)}) collective-permute-start(bf16[4,2,512,128]{3,2,1,0:T(8,128)(2,1)} %get-tuple-element.237.refs_1_), channel_id=1, source_target_pairs={{0,16},{8,24},{16,0},{24,8},{1,17},{9,25},{17,1},{25,9},{2,18},{10... | collective-permute-start | bytes 3145736 | tf_op jit(solution)/shard_map/ppermute | solution.py:345
  42.7 2.5 collective-permute-start.3
  43.5 10.7 collective-permute-start.4
  44.8 18.3 %collective-permute-start.5 = (bf16[1,3,512,128]{3,2,1,0:T(8,128)(2,1)S(1)}, bf16[1,3,512,128]{3,2,1,0:T(8,128)(2,1)S(1)}, u32[]{:S(2)}, u32[]{:S(2)}) collective-permute-start(bf16[1,3,512,128]{3,2,1,0:T(8,128)(2,1)S(1)} %copy-done.29), channel_id=1, source_target_pairs={{0,3},{1,2},{2,1},{3,0},{4,7},{5,6},{6,5},{7,4},{8,11},{9,10},{10,... | collective-permute-start | bytes 1179656 | tf_op jit(solution)/shard_map/ppermute | solution.py:345
  63.1 39.1 %collective-permute-start.8 = (bf16[1,3,512,128]{3,2,1,0:T(8,128)(2,1)S(1)}, bf16[1,3,512,128]{3,2,1,0:T(8,128)(2,1)S(1)}, u32[]{:S(2)}, u32[]{:S(2)}) collective-permute-start(bf16[1,3,512,128]{3,2,1,0:T(8,128)(2,1)S(1)} %copy-done.28), channel_id=1, source_target_pairs={{0,1},{1,0},{2,3},{3,2},{4,5},{5,4},{6,7},{7,6},{8,9},{9,8},{10,11... | collective-permute-start | bytes 1179656 | tf_op jit(solution)/shard_map/ppermute | solution.py:345
  63.1 40.5 %collective-permute-start.9 = (bf16[1,3,512,128]{3,2,1,0:T(8,128)(2,1)S(1)}, bf16[1,3,512,128]{3,2,1,0:T(8,128)(2,1)}, u32[]{:S(2)}, u32[]{:S(2)}) collective-permute-start(bf16[1,3,512,128]{3,2,1,0:T(8,128)(2,1)S(1)} %copy-done.27), channel_id=1, source_target_pairs={{0,2},{1,3},{2,0},{3,1},{4,6},{5,7},{6,4},{7,5},{8,10},{9,11},{10,... | collective-permute-start | bytes 1179656 | tf_op jit(solution)/shard_map/ppermute | solution.py:345
  64.4 39.2 %collective-permute-start.10 = (bf16[1,3,512,128]{3,2,1,0:T(8,128)(2,1)S(1)}, bf16[1,3,512,128]{3,2,1,0:T(8,128)(2,1)}, u32[]{:S(2)}, u32[]{:S(2)}) collective-permute-start(bf16[1,3,512,128]{3,2,1,0:T(8,128)(2,1)S(1)} %copy-done.26), channel_id=1, source_target_pairs={{0,3},{1,2},{2,1},{3,0},{4,7},{5,6},{6,5},{7,4},{8,11},{9,10},{10,... | collective-permute-start | bytes 1179656 | tf_op jit(solution)/shard_map/ppermute | solution.py:345
  65.2 53.2 %collective-permute-start.11 = (bf16[4,2,512,128]{3,2,1,0:T(8,128)(2,1)S(1)}, bf16[4,2,512,128]{3,2,1,0:T(8,128)(2,1)}, u32[]{:S(2)}, u32[]{:S(2)}) collective-permute-start(bf16[4,2,512,128]{3,2,1,0:T(8,128)(2,1)S(1)} %copy-done.10), channel_id=1, source_target_pairs={{0,4},{1,5},{2,6},{3,7},{4,0},{5,1},{6,2},{7,3},{8,12},{9,13},{10,... | collective-permute-start | bytes 3145736 | tf_op jit(solution)/shard_map/ppermute | solution.py:345
  80.8 41.2 %collective-permute-start.12 = (bf16[4,2,512,128]{3,2,1,0:T(8,128)(2,1)}, bf16[4,2,512,128]{3,2,1,0:T(8,128)(2,1)}, u32[]{:S(2)}, u32[]{:S(2)}) collective-permute-start(bf16[4,2,512,128]{3,2,1,0:T(8,128)(2,1)} %get-tuple-element.261.refs_1_), channel_id=1, source_target_pairs={{0,8},{8,0},{16,24},{24,16},{1,9},{9,1},{17,25},{25,17},{2,10},{10... | collective-permute-start | bytes 3145736 | tf_op jit(solution)/shard_map/ppermute | solution.py:345
  102.2 23.3 %collective-permute-start.13 = (bf16[4,2,512,128]{3,2,1,0:T(8,128)(2,1)}, bf16[4,2,512,128]{3,2,1,0:T(8,128)(2,1)S(1)}, u32[]{:S(2)}, u32[]{:S(2)}) collective-permute-start(bf16[4,2,512,128]{3,2,1,0:T(8,128)(2,1)} %get-tuple-element.261.refs_1_), channel_id=1, source_target_pairs={{0,16},{8,24},{16,0},{24,8},{1,17},{9,25},{17,1},{25,9},{2,18},{10... | collective-permute-start | bytes 3145736 | tf_op jit(solution)/shard_map/ppermute | solution.py:345
  116.8 23.2 %collective-permute-start.14 = (bf16[4,2,512,128]{3,2,1,0:T(8,128)(2,1)}, bf16[4,2,512,128]{3,2,1,0:T(8,128)(2,1)S(1)}, u32[]{:S(2)}, u32[]{:S(2)}) collective-permute-start(bf16[4,2,512,128]{3,2,1,0:T(8,128)(2,1)} %get-tuple-element.271.refs_1_), channel_id=1, source_target_pairs={{0,8},{8,0},{16,24},{24,16},{1,9},{9,1},{17,25},{25,17},{2,10},{10... | collective-permute-start | bytes 3145736 | tf_op jit(solution)/shard_map/ppermute | solution.py:345
  117.7 46.4 %collective-permute-start.15 = (bf16[4,2,512,128]{3,2,1,0:T(8,128)(2,1)}, bf16[4,2,512,128]{3,2,1,0:T(8,128)(2,1)S(1)}, u32[]{:S(2)}, u32[]{:S(2)}) collective-permute-start(bf16[4,2,512,128]{3,2,1,0:T(8,128)(2,1)} %get-tuple-element.271.refs_1_), channel_id=1, source_target_pairs={{0,16},{8,24},{16,0},{24,8},{1,17},{9,25},{17,1},{25,9},{2,18},{10... | collective-permute-start | bytes 3145736 | tf_op jit(solution)/shard_map/ppermute | solution.py:345
  118.4 47.4 %collective-permute-start.19 = (bf16[4,2,512,128]{3,2,1,0:T(8,128)(2,1)S(1)}, bf16[4,2,512,128]{3,2,1,0:T(8,128)(2,1)S(1)}, u32[]{:S(2)}, u32[]{:S(2)}) collective-permute-start(bf16[4,2,512,128]{3,2,1,0:T(8,128)(2,1)S(1)} %copy-done.4), channel_id=1, source_target_pairs={{0,4},{1,5},{2,6},{3,7},{4,0},{5,1},{6,2},{7,3},{8,12},{9,13},{10,... | collective-permute-start | bytes 3145736 | tf_op jit(solution)/shard_map/ppermute | solution.py:345
  125.5 60.9 %collective-permute-start.16 = (bf16[1,5,512,128]{3,2,1,0:T(8,128)(2,1)}, bf16[1,5,512,128]{3,2,1,0:T(8,128)(2,1)S(1)}, u32[]{:S(2)}, u32[]{:S(2)}) collective-permute-start(bf16[1,5,512,128]{3,2,1,0:T(8,128)(2,1)} %get-tuple-element.223), channel_id=1, source_target_pairs={{0,1},{1,0},{2,3},{3,2},{4,5},{5,4},{6,7},{7,6},{8,9},{9,8},{10,11... | collective-permute-start | bytes 1966088 | tf_op jit(solution)/shard_map/ppermute | solution.py:345
  130.2 56.3 %collective-permute-start.17 = (bf16[1,5,512,128]{3,2,1,0:T(8,128)(2,1)}, bf16[1,5,512,128]{3,2,1,0:T(8,128)(2,1)}, u32[]{:S(2)}, u32[]{:S(2)}) collective-permute-start(bf16[1,5,512,128]{3,2,1,0:T(8,128)(2,1)} %get-tuple-element.224), channel_id=1, source_target_pairs={{0,2},{1,3},{2,0},{3,1},{4,6},{5,7},{6,4},{7,5},{8,10},{9,11},{10,... | collective-permute-start | bytes 1966088 | tf_op jit(solution)/shard_map/ppermute | solution.py:345
  140.1 46.6 %collective-permute-start.18 = (bf16[1,5,512,128]{3,2,1,0:T(8,128)(2,1)}, bf16[1,5,512,128]{3,2,1,0:T(8,128)(2,1)}, u32[]{:S(2)}, u32[]{:S(2)}) collective-permute-start(bf16[1,5,512,128]{3,2,1,0:T(8,128)(2,1)} %get-tuple-element.225), channel_id=1, source_target_pairs={{0,3},{1,2},{2,1},{3,0},{4,7},{5,6},{6,5},{7,4},{8,11},{9,10},{10,... | collective-permute-start | bytes 1966088 | tf_op jit(solution)/shard_map/ppermute | solution.py:345
  165.8 46.8 %collective-permute-start.22 = (bf16[4,2,512,128]{3,2,1,0:T(8,128)(2,1)}, bf16[4,2,512,128]{3,2,1,0:T(8,128)(2,1)S(1)}, u32[]{:S(2)}, u32[]{:S(2)}) collective-permute-start(bf16[4,2,512,128]{3,2,1,0:T(8,128)(2,1)} %get-tuple-element.261.refs_1_), channel_id=1, source_target_pairs={{0,4},{1,5},{2,6},{3,7},{4,0},{5,1},{6,2},{7,3},{8,12},{9,13},{10,... | collective-permute-start | bytes 3145736 | tf_op jit(solution)/shard_map/ppermute | solution.py:345
  186.4 26.2 %copy-start.3 = (bf16[4,2,512,128]{3,2,1,0:T(8,128)(2,1)S(1)}, bf16[4,2,512,128]{3,2,1,0:T(8,128)(2,1)}, u32[]{:S(2)}) copy-start(bf16[4,2,512,128]{3,2,1,0:T(8,128)(2,1)} %get-tuple-element.271.refs_1_) | copy-start | bytes 3145732
  200.9 235.4 %collective-permute-start.20 = (bf16[4,2,512,128]{3,2,1,0:T(8,128)(2,1)}, bf16[4,2,512,128]{3,2,1,0:T(8,128)(2,1)S(1)}, u32[]{:S(2)}, u32[]{:S(2)}) collective-permute-start(bf16[4,2,512,128]{3,2,1,0:T(8,128)(2,1)} %get-tuple-element.251.refs_3_), channel_id=1, source_target_pairs={{0,8},{8,0},{16,24},{24,16},{1,9},{9,1},{17,25},{25,17},{2,10},{10... | collective-permute-start | bytes 3145736 | tf_op jit(solution)/shard_map/ppermute | solution.py:345
  201.4 234.9 %collective-permute-start.21 = (bf16[4,2,512,128]{3,2,1,0:T(8,128)(2,1)}, bf16[4,2,512,128]{3,2,1,0:T(8,128)(2,1)S(1)}, u32[]{:S(2)}, u32[]{:S(2)}) collective-permute-start(bf16[4,2,512,128]{3,2,1,0:T(8,128)(2,1)} %get-tuple-element.251.refs_3_), channel_id=1, source_target_pairs={{0,16},{8,24},{16,0},{24,8},{1,17},{9,25},{17,1},{25,9},{2,18},{10... | collective-permute-start | bytes 3145736 | tf_op jit(solution)/shard_map/ppermute | solution.py:345
  212.6 218.8 %copy-start.1 = (bf16[4,2,512,128]{3,2,1,0:T(8,128)(2,1)}, bf16[4,2,512,128]{3,2,1,0:T(8,128)(2,1)S(1)}, u32[]{:S(2)}) copy-start(bf16[4,2,512,128]{3,2,1,0:T(8,128)(2,1)S(1)} %collective-permute-done.22.refs_0_.refs_4_) | copy-start | bytes 3145732
  212.6 681.0 %collective-permute-start.23 = (bf16[4,2,512,128]{3,2,1,0:T(8,128)(2,1)S(1)}, bf16[4,2,512,128]{3,2,1,0:T(8,128)(2,1)S(1)}, u32[]{:S(2)}, u32[]{:S(2)}) collective-permute-start(bf16[4,2,512,128]{3,2,1,0:T(8,128)(2,1)S(1)} %copy-done.3), channel_id=1, source_target_pairs={{0,4},{1,5},{2,6},{3,7},{4,0},{5,1},{6,2},{7,3},{8,12},{9,13},{10,... | collective-permute-start | bytes 3145736 | tf_op jit(solution)/shard_map/ppermute | solution.py:345
  431.4 463.4 %collective-permute-start.27 = (bf16[512,128]{1,0:T(8,128)(2,1)}, bf16[512,128]{1,0:T(8,128)(2,1)S(1)}, u32[]{:S(2)}, u32[]{:S(2)}) collective-permute-start(bf16[512,128]{1,0:T(8,128)(2,1)} %get-tuple-element.279), channel_id=1, source_target_pairs={{0,1},{1,0},{2,3},{3,2},{4,5},{5,4},{6,7},{7,6},{8,9},{9,8},{10,11... | collective-permute-start | bytes 393224 | tf_op jit(solution)/shard_map/ppermute | solution.py:345
  433.9 461.7 %collective-permute-start.28 = (bf16[512,128]{1,0:T(8,128)(2,1)}, bf16[512,128]{1,0:T(8,128)(2,1)S(1)}, u32[]{:S(2)}, u32[]{:S(2)}) collective-permute-start(bf16[512,128]{1,0:T(8,128)(2,1)} %get-tuple-element.280), channel_id=1, source_target_pairs={{0,2},{1,3},{2,0},{3,1},{4,6},{5,7},{6,4},{7,5},{8,10},{9,11},{10,... | collective-permute-start | bytes 393224 | tf_op jit(solution)/shard_map/ppermute | solution.py:345
  436.3 459.4 %collective-permute-start.29 = (bf16[512,128]{1,0:T(8,128)(2,1)}, bf16[512,128]{1,0:T(8,128)(2,1)S(1)}, u32[]{:S(2)}, u32[]{:S(2)}) collective-permute-start(bf16[512,128]{1,0:T(8,128)(2,1)} %get-tuple-element.281), channel_id=1, source_target_pairs={{0,3},{1,2},{2,1},{3,0},{4,7},{5,6},{6,5},{7,4},{8,11},{9,10},{10,... | collective-permute-start | bytes 393224 | tf_op jit(solution)/shard_map/ppermute | solution.py:345
  674.7 222.3 %collective-permute-start.33 = (bf16[512,128]{1,0:T(8,128)(2,1)}, bf16[512,128]{1,0:T(8,128)(2,1)S(1)}, u32[]{:S(2)}, u32[]{:S(2)}) collective-permute-start(bf16[512,128]{1,0:T(8,128)(2,1)} %get-tuple-element.285), channel_id=1, source_target_pairs={{0,1},{1,0},{2,3},{3,2},{4,5},{5,4},{6,7},{7,6},{8,9},{9,8},{10,11... | collective-permute-start | bytes 393224 | tf_op jit(solution)/shard_map/ppermute | solution.py:345
  675.1 218.5 %copy-start.40 = (bf16[512,128]{1,0:T(8,128)(2,1)S(1)}, bf16[512,128]{1,0:T(8,128)(2,1)}, u32[]{:S(2)}) copy-start(bf16[512,128]{1,0:T(8,128)(2,1)} %get-tuple-element.286) | copy-start | bytes 393220
  675.1 219.7 %copy-start.39 = (bf16[512,128]{1,0:T(8,128)(2,1)S(1)}, bf16[512,128]{1,0:T(8,128)(2,1)}, u32[]{:S(2)}) copy-start(bf16[512,128]{1,0:T(8,128)(2,1)} %get-tuple-element.287) | copy-start | bytes 393220
  893.6 222.6 %collective-permute-start.34 = (bf16[512,128]{1,0:T(8,128)(2,1)S(1)}, bf16[512,128]{1,0:T(8,128)(2,1)S(1)}, u32[]{:S(2)}, u32[]{:S(2)}) collective-permute-start(bf16[512,128]{1,0:T(8,128)(2,1)S(1)} %copy-done.40), channel_id=1, source_target_pairs={{0,2},{1,3},{2,0},{3,1},{4,6},{5,7},{6,4},{7,5},{8,10},{9,11},{10,... | collective-permute-start | bytes 393224 | tf_op jit(solution)/shard_map/ppermute | solution.py:345
  894.9 221.3 %copy-start.11 = (bf16[512,128]{1,0:T(8,128)(2,1)}, bf16[512,128]{1,0:T(8,128)(2,1)S(1)}, u32[]{:S(2)}) copy-start(bf16[512,128]{1,0:T(8,128)(2,1)S(1)} %collective-permute-done.27.refs_1_) | copy-start | bytes 393220
  894.9 221.5 %collective-permute-start.35 = (bf16[512,128]{1,0:T(8,128)(2,1)S(1)}, bf16[512,128]{1,0:T(8,128)(2,1)S(1)}, u32[]{:S(2)}, u32[]{:S(2)}) collective-permute-start(bf16[512,128]{1,0:T(8,128)(2,1)S(1)} %copy-done.39), channel_id=1, source_target_pairs={{0,3},{1,2},{2,1},{3,0},{4,7},{5,6},{6,5},{7,4},{8,11},{9,10},{10,... | collective-permute-start | bytes 393224 | tf_op jit(solution)/shard_map/ppermute | solution.py:345
  895.6 220.6 %copy-start.12 = (bf16[512,128]{1,0:T(8,128)(2,1)}, bf16[512,128]{1,0:T(8,128)(2,1)S(1)}, u32[]{:S(2)}) copy-start(bf16[512,128]{1,0:T(8,128)(2,1)S(1)} %collective-permute-done.28.refs_2_) | copy-start | bytes 393220
  895.6 222.2 %collective-permute-start.30 = (bf16[512,128]{1,0:T(8,128)(2,1)}, bf16[512,128]{1,0:T(8,128)(2,1)S(1)}, u32[]{:S(2)}, u32[]{:S(2)}) collective-permute-start(bf16[512,128]{1,0:T(8,128)(2,1)} %get-tuple-element.282), channel_id=1, source_target_pairs={{0,1},{1,0},{2,3},{3,2},{4,5},{5,4},{6,7},{7,6},{8,9},{9,8},{10,11... | collective-permute-start | bytes 393224 | tf_op jit(solution)/shard_map/ppermute | solution.py:345
  895.7 220.5 %copy-start.13 = (bf16[512,128]{1,0:T(8,128)(2,1)}, bf16[512,128]{1,0:T(8,128)(2,1)S(1)}, u32[]{:S(2)}) copy-start(bf16[512,128]{1,0:T(8,128)(2,1)S(1)} %collective-permute-done.29.refs_3_) | copy-start | bytes 393220
  895.7 222.8 %collective-permute-start.31 = (bf16[512,128]{1,0:T(8,128)(2,1)}, bf16[512,128]{1,0:T(8,128)(2,1)S(1)}, u32[]{:S(2)}, u32[]{:S(2)}) collective-permute-start(bf16[512,128]{1,0:T(8,128)(2,1)} %get-tuple-element.283), channel_id=1, source_target_pairs={{0,2},{1,3},{2,0},{3,1},{4,6},{5,7},{6,4},{7,5},{8,10},{9,11},{10,... | collective-permute-start | bytes 393224 | tf_op jit(solution)/shard_map/ppermute | solution.py:345
  897.0 219.2 %copy-start.14 = (bf16[512,128]{1,0:T(8,128)(2,1)}, bf16[512,128]{1,0:T(8,128)(2,1)S(1)}, u32[]{:S(2)}) copy-start(bf16[512,128]{1,0:T(8,128)(2,1)S(1)} %collective-permute-done.33.refs_9_) | copy-start | bytes 393220
  897.0 221.4 %collective-permute-start.32 = (bf16[512,128]{1,0:T(8,128)(2,1)}, bf16[512,128]{1,0:T(8,128)(2,1)S(1)}, u32[]{:S(2)}, u32[]{:S(2)}) collective-permute-start(bf16[512,128]{1,0:T(8,128)(2,1)} %get-tuple-element.284), channel_id=1, source_target_pairs={{0,3},{1,2},{2,1},{3,0},{4,7},{5,6},{6,5},{7,4},{8,11},{9,10},{10,... | collective-permute-start | bytes 393224 | tf_op jit(solution)/shard_map/ppermute | solution.py:345
  1116.2 5.5 collective-permute-start.24
  1116.4 5.4 collective-permute-start.25
  1117.8 6.9 collective-permute-start.26
  (29 other events, 225.2 us)

commit v3 on v2

--- a/solution.py
+++ b/solution.py
@@ -209,17 +209,16 @@
 
 def more_kernel(qe_ref, acc_ref, *refs, n_refs, n):
     kv_refs, (out_ref, keys_ref, values_ref) = refs[:n_refs], refs[n_refs:]
-    h = pl.program_id(1)
-
-    @pl.when((pl.program_id(0) == 0) & (h == 0))
+
+    @pl.when(pl.program_id(0) == 0)
     def _():
         prepare(kv_refs, keys_ref, values_ref)
 
-    query = qe_ref[0]
-    out_ref[0] = acc_ref[0]
+    out_ref[...] = acc_ref[...]
 
     def step(slot, carry):
-        out_ref[0] += weigh(keys_ref[slot, h], values_ref[slot, h], query)
+        for h in range(2):
+            out_ref[h] += weigh(keys_ref[slot, h], values_ref[slot, h], qe_ref[h])
         return carry
 
     lax.fori_loop(0, n, step, 0)
@@ -229,12 +228,12 @@
     tokens = qe.shape[1]
     n = blocks_of(kvs, tokens)
     tile = kvs[0].shape[2]
-    state = pl.BlockSpec((1, HEAD_ROWS, tile), lambda i, h: (h, 0, i))
+    state = pl.BlockSpec((2, HEAD_ROWS, tile), lambda i: (0, 0, i))
     return pl.pallas_call(
         functools.partial(more_kernel, n_refs=len(kvs), n=n),
-        grid=(tokens // tile, 2),
-        in_specs=[pl.BlockSpec((1, tile, LANES), lambda i, h: (h, i, 0)), state]
-        + [pl.BlockSpec(kv.shape, lambda i, h: (0, 0, 0, 0)) for kv in kvs],
+        grid=(tokens // tile,),
+        in_specs=[pl.BlockSpec((2, tile, LANES), lambda i: (0, i, 0)), state]
+        + [pl.BlockSpec(kv.shape, lambda i: (0, 0, 0, 0)) for kv in kvs],
         out_specs=state,
         out_shape=jax.ShapeDtypeStruct(acc.shape, F32),
         scratch_shapes=[

time: 1140 us -> 1140 us (level)
  no operation moved by 1% of the time
where the time goes in v3:
time: 1140 us; the launch traced here: 1130 us
  Pallas kernels  1020 us (89%)
  waiting for transfers between devices  60.4 us (5%)
  starting transfers between devices  39.8 us (3%)
    pallas_call x4, Pallas kernels, last(): pl.pallas_call(functools.partial(last_kernel, n_refs=len(kvs), n_all=n_al...  893 us
    ppermute x36, waiting for transfers between devices, swap(): return lax.ppermute(x, axis, [(i, i ^ bit) for i in range(size)])  60.4 us
    pallas_call x3, Pallas kernels, more(): pl.pallas_call(functools.partial(more_kernel, n_refs=len(kvs), n=n), grid...  57.2 us
    pallas_call x4, Pallas kernels, first(): pl.pallas_call(functools.partial(first_kernel, n=n, kinds=kinds), grid=(n...  53.6 us
    ppermute x36, starting transfers between devices, swap(): return lax.ppermute(x, axis, [(i, i ^ bit) for i in range(size)])  39.8 us
  transfers between devices with their start and end apart: 36, of which 10 were waited for; matrix products, arithmetic and copies ran while one was open for 0% of the time, Pallas kernels for 89%

profile of v3, /device:TPU:1, one launch (start us, length us, event | category | flops | bytes accessed | tf_op | source)
XLA Modules:
  0.0 1126.0 jit_solution(17347996492810171817)
XLA Ops:
  0.0 2.3 shard_map.17
  2.3 2.6 shard_map.18
  5.1 2.8 collective-permute-start.1
  7.9 2.7 shard_map.19
  10.5 2.7 shard_map.20
  13.3 4.1 collective-permute-done.1.refs_2_
  17.4 8.4 collective-permute-done.2.refs_3_
  26.6 13.4 %shard_map.21 = (bf16[4,2,512,128]{3,2,1,0:T(8,128)(2,1)}, bf16[2,2048,128]{2,1,0:T(8,128)(2,1)}, f32[2,80,2048]{2,1,0:T(8,128)}) custom-call(s32[1]{0:T(128)} %bitcast.rank_ref, bf16[1,3,512,128]{3,2,1,0:T(8,128)(2,1)} %get-tuple-element.169.refs_0_, bf16[1,3,512,128]{3,2,1,0:T(8,128)(2,1)} %copy-done.36, bf16[1,3,512,128]{3,2,1,0:T(8,128)(2,1)} %copy-done.37, ...), custom_call_target="tpu_custom_call" | custom-call | flops 2000000000 | bytes 1048576 | tf_op jit(solution)/shard_map/pallas_call | solution.py:183
  40.1 1.4 collective-permute-start.6
  41.4 1.2 collective-permute-start.7
  42.7 0.8 collective-permute-start.3
  43.5 1.3 collective-permute-start.4
  45.2 9.0 collective-permute-done.4.refs_2_
  54.2 8.9 collective-permute-done.5.refs_3_
  63.1 1.3 collective-permute-start.9
  65.2 2.3 collective-permute-start.11
  67.6 13.2 %shard_map.22 = (bf16[4,2,512,128]{3,2,1,0:T(8,128)(2,1)}, bf16[2,2048,128]{2,1,0:T(8,128)(2,1)}, f32[2,80,2048]{2,1,0:T(8,128)}) custom-call(s32[1]{0:T(128)} %bitcast.rank_ref, bf16[1,3,512,128]{3,2,1,0:T(8,128)(2,1)} %get-tuple-element.182.refs_0_, bf16[1,3,512,128]{3,2,1,0:T(8,128)(2,1)} %copy-done.33, bf16[1,3,512,128]{3,2,1,0:T(8,128)(2,1)} %copy-done.34, ...), custom_call_target="tpu_custom_call" | custom-call | flops 2000000000 | bytes 1048576 | tf_op jit(solution)/shard_map/pallas_call | solution.py:183
  80.8 1.1 collective-permute-start.12
  81.9 18.9 %shard_map.23.acc_ref = f32[2,80,2048]{2,1,0:T(8,128)} custom-call(bf16[2,2048,128]{2,1,0:T(8,128)(2,1)} %get-tuple-element.234.qe_ref, f32[2,80,2048]{2,1,0:T(8,128)} %get-tuple-element.190.acc_ref, bf16[4,2,512,128]{3,2,1,0:T(8,128)(2,1)} %copy-done.6, bf16[4,2,512,128]{3,2,1,0:T(8,128)(2,1)} %copy-done.8), custom_call_target="tpu_custom_call", output_to_operand_aliasing={{}: (1, {})} | custom-call | flops 4000000000 | bytes 1048576 | tf_op jit(solution)/shard_map/pallas_call | solution.py:232
  100.9 1.4 collective-permute-start.13
  102.3 13.3 %shard_map.24 = (bf16[4,2,512,128]{3,2,1,0:T(8,128)(2,1)}, bf16[2,2048,128]{2,1,0:T(8,128)(2,1)}, f32[2,80,2048]{2,1,0:T(8,128)}) custom-call(s32[1]{0:T(128)} %bitcast.rank_ref, bf16[1,3,512,128]{3,2,1,0:T(8,128)(2,1)} %get-tuple-element.201.refs_0_, bf16[1,3,512,128]{3,2,1,0:T(8,128)(2,1)} %copy-done.30, ...), custom_call_target="tpu_custom_call" | custom-call | flops 2000000000 | bytes 1048576 | tf_op jit(solution)/shard_map/pallas_call | solution.py:183
  115.6 0.9 collective-permute-start.14
  117.4 3.3 shard_map.25
  120.7 3.5 collective-permute-done.13.refs_1_.refs_3_
  124.2 4.6 collective-permute-start.16
  128.9 1.3 collective-permute-start.17
  130.2 8.7 collective-permute-done.14.refs_0_.refs_2_
  138.8 3.7 collective-permute-start.18
  142.6 19.0 %shard_map.26.acc_ref = f32[2,80,2048]{2,1,0:T(8,128)} custom-call(bf16[2,2048,128]{2,1,0:T(8,128)(2,1)} %get-tuple-element.258.qe_ref, f32[2,80,2048]{2,1,0:T(8,128)} %get-tuple-element.214.acc_ref, bf16[4,2,512,128]{3,2,1,0:T(8,128)(2,1)} %collective-permute-done.12.refs_0_.refs_2_, bf16[4,2,512,128]{3,2,1,0:T(8,128)(2,1)} %copy-done.9), custom_call_target="tpu_custom_call", output_to_operand_aliasing={{}: (1, {})} | custom-call | flops 4000000000 | bytes 1048576 | tf_op jit(solution)/shard_map/pallas_call | solution.py:232
  161.6 2.9 collective-permute-done.19.refs_0_.refs_4_
  164.5 19.3 %shard_map.27.acc_ref = f32[2,80,2048]{2,1,0:T(8,128)} custom-call(bf16[2,2048,128]{2,1,0:T(8,128)(2,1)} %get-tuple-element.268.qe_ref, f32[2,80,2048]{2,1,0:T(8,128)} %get-tuple-element.220.acc_ref, bf16[4,2,512,128]{3,2,1,0:T(8,128)(2,1)} %copy-done.5, bf16[4,2,512,128]{3,2,1,0:T(8,128)(2,1)} %copy-done.7), custom_call_target="tpu_custom_call", output_to_operand_aliasing={{}: (1, {})} | custom-call | flops 4000000000 | bytes 1048576 | tf_op jit(solution)/shard_map/pallas_call | solution.py:232
  183.8 1.5 collective-permute-done.18.refs_3_
  185.3 13.7 %shard_map.28 = (bf16[4,2,512,128]{3,2,1,0:T(8,128)(2,1)}, bf16[4,2,512,128]{3,2,1,0:T(8,128)(2,1)}, bf16[2,2048,128]{2,1,0:T(8,128)(2,1)}, f32[2,80,2048]{2,1,0:T(8,128)}) custom-call(s32[1]{0:T(128)} %bitcast.rank_ref, bf16[1,5,512,128]{3,2,1,0:T(8,128)(2,1)} %get-tuple-element.227.refs_0_, bf16[1,5,512,128]{3,2,1,0:T(8,128)(2,1)} %copy-done.25, ...), custom_call_target="tpu_custom_call" | custom-call | flops 2000000000 | bytes 1048576 | tf_op jit(solution)/shard_map/pallas_call | solution.py:183
  199.6 1.2 collective-permute-start.21
  200.8 10.5 collective-permute-done.22.refs_0_.refs_4_
  211.3 218.8 %shard_map.29 = (bf16[512,128]{1,0:T(8,128)(2,1)}, bf16[512,128]{1,0:T(8,128)(2,1)}, bf16[512,128]{1,0:T(8,128)(2,1)}, bf16[512,128]{1,0:T(8,128)(2,1)}) custom-call(s32[1]{0:T(128)} %bitcast.rank_ref, bf16[2,2048,128]{2,1,0:T(8,128)(2,1)} %get-tuple-element.234.qe_ref, f32[2,80,2048]{2,1,0:T(8,128)} %shard_map.23.acc_ref, ...), custom_call_target="tpu_custom_call" | custom-call | flops 2000000000 | bytes 1048576 | tf_op jit(solution)/shard_map/pallas_call | solution.py:317
  430.1 2.4 collective-permute-start.27
  432.5 2.4 collective-permute-start.28
  435.0 0.9 copy-done.23
  436.3 237.1 %shard_map.30 = (bf16[512,128]{1,0:T(8,128)(2,1)}, bf16[512,128]{1,0:T(8,128)(2,1)}, bf16[512,128]{1,0:T(8,128)(2,1)}, bf16[512,128]{1,0:T(8,128)(2,1)}) custom-call(s32[1]{0:T(128)} %bitcast.rank_ref, bf16[2,2048,128]{2,1,0:T(8,128)(2,1)} %get-tuple-element.246.qe_ref, f32[2,80,2048]{2,1,0:T(8,128)} %get-tuple-element.247.acc_ref, ...), custom_call_target="tpu_custom_call" | custom-call | flops 6000000000 | bytes 1048576 | tf_op jit(solution)/shard_map/pallas_call | solution.py:317
  673.8 218.4 %shard_map.31 = (bf16[512,128]{1,0:T(8,128)(2,1)}, bf16[512,128]{1,0:T(8,128)(2,1)}, bf16[512,128]{1,0:T(8,128)(2,1)}, bf16[512,128]{1,0:T(8,128)(2,1)}) custom-call(s32[1]{0:T(128)} %bitcast.rank_ref, bf16[2,2048,128]{2,1,0:T(8,128)(2,1)} %get-tuple-element.258.qe_ref, f32[2,80,2048]{2,1,0:T(8,128)} %shard_map.26.acc_ref, ...), custom_call_target="tpu_custom_call" | custom-call | flops 2000000000 | bytes 1048576 | tf_op jit(solution)/shard_map/pallas_call | solution.py:317
  892.3 1.2 collective-permute-start.34
  894.3 1.3 collective-permute-start.31
  896.4 218.4 %shard_map.32 = (bf16[512,128]{1,0:T(8,128)(2,1)}, bf16[512,128]{1,0:T(8,128)(2,1)}, bf16[512,128]{1,0:T(8,128)(2,1)}, bf16[512,128]{1,0:T(8,128)(2,1)}) custom-call(s32[1]{0:T(128)} %bitcast.rank_ref, bf16[2,2048,128]{2,1,0:T(8,128)(2,1)} %get-tuple-element.268.qe_ref, f32[2,80,2048]{2,1,0:T(8,128)} %shard_map.27.acc_ref, bf16[4,2,512,128]{3,2,1,0:T(8,128)(2,1)} %copy-done, ...), custom_call_target="tpu_custom_call" | custom-call | flops 2000000000 | bytes 1048576 | tf_op jit(solution)/shard_map/pallas_call | solution.py:317
  1115.0 1.4 collective-permute-start.25
  1117.8 2.6 shard_map.33.refs_4_
  1120.4 2.9 collective-permute-done.26.refs_3_
  1124.0 1.9 shard_map.34
  (124 shorter events, 8.4 us)
Async XLA Ops:
  4.9 8.3 collective-permute-start
  5.1 12.4 %collective-permute-start.1 = (bf16[1,3,512,128]{3,2,1,0:T(8,128)(2,1)}, bf16[1,3,512,128]{3,2,1,0:T(8,128)(2,1)S(1)}, u32[]{:S(2)}, u32[]{:S(2)}) collective-permute-start(bf16[1,3,512,128]{3,2,1,0:T(8,128)(2,1)} %get-tuple-element.166), channel_id=1, source_target_pairs={{0,2},{1,3},{2,0},{3,1},{4,6},{5,7},{6,4},{7,5},{8,10},{9,11},{10,... | collective-permute-start | bytes 1179656 | tf_op jit(solution)/shard_map/ppermute | solution.py:344
  7.8 18.0 %collective-permute-start.2 = (bf16[1,3,512,128]{3,2,1,0:T(8,128)(2,1)}, bf16[1,3,512,128]{3,2,1,0:T(8,128)(2,1)S(1)}, u32[]{:S(2)}, u32[]{:S(2)}) collective-permute-start(bf16[1,3,512,128]{3,2,1,0:T(8,128)(2,1)} %get-tuple-element.167), channel_id=1, source_target_pairs={{0,3},{1,2},{2,1},{3,0},{4,7},{5,6},{6,5},{7,4},{8,11},{9,10},{10,... | collective-permute-start | bytes 1179656 | tf_op jit(solution)/shard_map/ppermute | solution.py:344
  26.6 36.5 %copy-start.28 = (bf16[1,3,512,128]{3,2,1,0:T(8,128)(2,1)S(1)}, bf16[1,3,512,128]{3,2,1,0:T(8,128)(2,1)}, u32[]{:S(2)}) copy-start(bf16[1,3,512,128]{3,2,1,0:T(8,128)(2,1)} %get-tuple-element.197) | copy-start | bytes 1179652
  26.6 36.5 %copy-start.27 = (bf16[1,3,512,128]{3,2,1,0:T(8,128)(2,1)S(1)}, bf16[1,3,512,128]{3,2,1,0:T(8,128)(2,1)}, u32[]{:S(2)}) copy-start(bf16[1,3,512,128]{3,2,1,0:T(8,128)(2,1)} %get-tuple-element.198) | copy-start | bytes 1179652
  26.6 37.8 %copy-start.26 = (bf16[1,3,512,128]{3,2,1,0:T(8,128)(2,1)S(1)}, bf16[1,3,512,128]{3,2,1,0:T(8,128)(2,1)}, u32[]{:S(2)}) copy-start(bf16[1,3,512,128]{3,2,1,0:T(8,128)(2,1)} %get-tuple-element.199) | copy-start | bytes 1179652
  26.6 38.6 %copy-start.10 = (bf16[4,2,512,128]{3,2,1,0:T(8,128)(2,1)S(1)}, bf16[4,2,512,128]{3,2,1,0:T(8,128)(2,1)}, u32[]{:S(2)}) copy-start(bf16[4,2,512,128]{3,2,1,0:T(8,128)(2,1)} %shard_map.17) | copy-start | bytes 3145732
  40.1 25.1 %collective-permute-start.6 = (bf16[4,2,512,128]{3,2,1,0:T(8,128)(2,1)}, bf16[4,2,512,128]{3,2,1,0:T(8,128)(2,1)S(1)}, u32[]{:S(2)}, u32[]{:S(2)}) collective-permute-start(bf16[4,2,512,128]{3,2,1,0:T(8,128)(2,1)} %get-tuple-element.237.refs_1_), channel_id=1, source_target_pairs={{0,8},{8,0},{16,24},{24,16},{1,9},{9,1},{17,25},{25,17},{2,10},{10... | collective-permute-start | bytes 3145736 | tf_op jit(solution)/shard_map/ppermute | solution.py:344
  41.4 39.4 %collective-permute-start.7 = (bf16[4,2,512,128]{3,2,1,0:T(8,128)(2,1)}, bf16[4,2,512,128]{3,2,1,0:T(8,128)(2,1)S(1)}, u32[]{:S(2)}, u32[]{:S(2)}) collective-permute-start(bf16[4,2,512,128]{3,2,1,0:T(8,128)(2,1)} %get-tuple-element.237.refs_1_), channel_id=1, source_target_pairs={{0,16},{8,24},{16,0},{24,8},{1,17},{9,25},{17,1},{25,9},{2,18},{10... | collective-permute-start | bytes 3145736 | tf_op jit(solution)/shard_map/ppermute | solution.py:344
  42.7 2.5 collective-permute-start.3
  43.5 10.7 collective-permute-start.4
  44.8 18.3 %collective-permute-start.5 = (bf16[1,3,512,128]{3,2,1,0:T(8,128)(2,1)S(1)}, bf16[1,3,512,128]{3,2,1,0:T(8,128)(2,1)S(1)}, u32[]{:S(2)}, u32[]{:S(2)}) collective-permute-start(bf16[1,3,512,128]{3,2,1,0:T(8,128)(2,1)S(1)} %copy-done.29), channel_id=1, source_target_pairs={{0,3},{1,2},{2,1},{3,0},{4,7},{5,6},{6,5},{7,4},{8,11},{9,10},{10,... | collective-permute-start | bytes 1179656 | tf_op jit(solution)/shard_map/ppermute | solution.py:344
  63.1 37.8 %collective-permute-start.8 = (bf16[1,3,512,128]{3,2,1,0:T(8,128)(2,1)S(1)}, bf16[1,3,512,128]{3,2,1,0:T(8,128)(2,1)S(1)}, u32[]{:S(2)}, u32[]{:S(2)}) collective-permute-start(bf16[1,3,512,128]{3,2,1,0:T(8,128)(2,1)S(1)} %copy-done.28), channel_id=1, source_target_pairs={{0,1},{1,0},{2,3},{3,2},{4,5},{5,4},{6,7},{7,6},{8,9},{9,8},{10,11... | collective-permute-start | bytes 1179656 | tf_op jit(solution)/shard_map/ppermute | solution.py:344
  63.1 39.2 %collective-permute-start.9 = (bf16[1,3,512,128]{3,2,1,0:T(8,128)(2,1)S(1)}, bf16[1,3,512,128]{3,2,1,0:T(8,128)(2,1)}, u32[]{:S(2)}, u32[]{:S(2)}) collective-permute-start(bf16[1,3,512,128]{3,2,1,0:T(8,128)(2,1)S(1)} %copy-done.27), channel_id=1, source_target_pairs={{0,2},{1,3},{2,0},{3,1},{4,6},{5,7},{6,4},{7,5},{8,10},{9,11},{10,... | collective-permute-start | bytes 1179656 | tf_op jit(solution)/shard_map/ppermute | solution.py:344
  64.4 37.9 %collective-permute-start.10 = (bf16[1,3,512,128]{3,2,1,0:T(8,128)(2,1)S(1)}, bf16[1,3,512,128]{3,2,1,0:T(8,128)(2,1)}, u32[]{:S(2)}, u32[]{:S(2)}) collective-permute-start(bf16[1,3,512,128]{3,2,1,0:T(8,128)(2,1)S(1)} %copy-done.26), channel_id=1, source_target_pairs={{0,3},{1,2},{2,1},{3,0},{4,7},{5,6},{6,5},{7,4},{8,11},{9,10},{10,... | collective-permute-start | bytes 1179656 | tf_op jit(solution)/shard_map/ppermute | solution.py:344
  65.2 51.8 %collective-permute-start.11 = (bf16[4,2,512,128]{3,2,1,0:T(8,128)(2,1)S(1)}, bf16[4,2,512,128]{3,2,1,0:T(8,128)(2,1)}, u32[]{:S(2)}, u32[]{:S(2)}) collective-permute-start(bf16[4,2,512,128]{3,2,1,0:T(8,128)(2,1)S(1)} %copy-done.10), channel_id=1, source_target_pairs={{0,4},{1,5},{2,6},{3,7},{4,0},{5,1},{6,2},{7,3},{8,12},{9,13},{10,... | collective-permute-start | bytes 3145736 | tf_op jit(solution)/shard_map/ppermute | solution.py:344
  80.8 39.8 %collective-permute-start.12 = (bf16[4,2,512,128]{3,2,1,0:T(8,128)(2,1)}, bf16[4,2,512,128]{3,2,1,0:T(8,128)(2,1)}, u32[]{:S(2)}, u32[]{:S(2)}) collective-permute-start(bf16[4,2,512,128]{3,2,1,0:T(8,128)(2,1)} %get-tuple-element.261.refs_1_), channel_id=1, source_target_pairs={{0,8},{8,0},{16,24},{24,16},{1,9},{9,1},{17,25},{25,17},{2,10},{10... | collective-permute-start | bytes 3145736 | tf_op jit(solution)/shard_map/ppermute | solution.py:344
  100.9 23.3 %collective-permute-start.13 = (bf16[4,2,512,128]{3,2,1,0:T(8,128)(2,1)}, bf16[4,2,512,128]{3,2,1,0:T(8,128)(2,1)S(1)}, u32[]{:S(2)}, u32[]{:S(2)}) collective-permute-start(bf16[4,2,512,128]{3,2,1,0:T(8,128)(2,1)} %get-tuple-element.261.refs_1_), channel_id=1, source_target_pairs={{0,16},{8,24},{16,0},{24,8},{1,17},{9,25},{17,1},{25,9},{2,18},{10... | collective-permute-start | bytes 3145736 | tf_op jit(solution)/shard_map/ppermute | solution.py:344
  115.6 23.3 %collective-permute-start.14 = (bf16[4,2,512,128]{3,2,1,0:T(8,128)(2,1)}, bf16[4,2,512,128]{3,2,1,0:T(8,128)(2,1)S(1)}, u32[]{:S(2)}, u32[]{:S(2)}) collective-permute-start(bf16[4,2,512,128]{3,2,1,0:T(8,128)(2,1)} %get-tuple-element.271.refs_1_), channel_id=1, source_target_pairs={{0,8},{8,0},{16,24},{24,16},{1,9},{9,1},{17,25},{25,17},{2,10},{10... | collective-permute-start | bytes 3145736 | tf_op jit(solution)/shard_map/ppermute | solution.py:344
  116.4 45.1 %collective-permute-start.15 = (bf16[4,2,512,128]{3,2,1,0:T(8,128)(2,1)}, bf16[4,2,512,128]{3,2,1,0:T(8,128)(2,1)S(1)}, u32[]{:S(2)}, u32[]{:S(2)}) collective-permute-start(bf16[4,2,512,128]{3,2,1,0:T(8,128)(2,1)} %get-tuple-element.271.refs_1_), channel_id=1, source_target_pairs={{0,16},{8,24},{16,0},{24,8},{1,17},{9,25},{17,1},{25,9},{2,18},{10... | collective-permute-start | bytes 3145736 | tf_op jit(solution)/shard_map/ppermute | solution.py:344
  117.1 47.4 %collective-permute-start.19 = (bf16[4,2,512,128]{3,2,1,0:T(8,128)(2,1)S(1)}, bf16[4,2,512,128]{3,2,1,0:T(8,128)(2,1)S(1)}, u32[]{:S(2)}, u32[]{:S(2)}) collective-permute-start(bf16[4,2,512,128]{3,2,1,0:T(8,128)(2,1)S(1)} %copy-done.4), channel_id=1, source_target_pairs={{0,4},{1,5},{2,6},{3,7},{4,0},{5,1},{6,2},{7,3},{8,12},{9,13},{10,... | collective-permute-start | bytes 3145736 | tf_op jit(solution)/shard_map/ppermute | solution.py:344
  124.2 59.5 %collective-permute-start.16 = (bf16[1,5,512,128]{3,2,1,0:T(8,128)(2,1)}, bf16[1,5,512,128]{3,2,1,0:T(8,128)(2,1)S(1)}, u32[]{:S(2)}, u32[]{:S(2)}) collective-permute-start(bf16[1,5,512,128]{3,2,1,0:T(8,128)(2,1)} %get-tuple-element.223), channel_id=1, source_target_pairs={{0,1},{1,0},{2,3},{3,2},{4,5},{5,4},{6,7},{7,6},{8,9},{9,8},{10,11... | collective-permute-start | bytes 1966088 | tf_op jit(solution)/shard_map/ppermute | solution.py:344
  128.9 54.9 %collective-permute-start.17 = (bf16[1,5,512,128]{3,2,1,0:T(8,128)(2,1)}, bf16[1,5,512,128]{3,2,1,0:T(8,128)(2,1)}, u32[]{:S(2)}, u32[]{:S(2)}) collective-permute-start(bf16[1,5,512,128]{3,2,1,0:T(8,128)(2,1)} %get-tuple-element.224), channel_id=1, source_target_pairs={{0,2},{1,3},{2,0},{3,1},{4,6},{5,7},{6,4},{7,5},{8,10},{9,11},{10,... | collective-permute-start | bytes 1966088 | tf_op jit(solution)/shard_map/ppermute | solution.py:344
  138.8 46.5 %collective-permute-start.18 = (bf16[1,5,512,128]{3,2,1,0:T(8,128)(2,1)}, bf16[1,5,512,128]{3,2,1,0:T(8,128)(2,1)}, u32[]{:S(2)}, u32[]{:S(2)}) collective-permute-start(bf16[1,5,512,128]{3,2,1,0:T(8,128)(2,1)} %get-tuple-element.225), channel_id=1, source_target_pairs={{0,3},{1,2},{2,1},{3,0},{4,7},{5,6},{6,5},{7,4},{8,11},{9,10},{10,... | collective-permute-start | bytes 1966088 | tf_op jit(solution)/shard_map/ppermute | solution.py:344
  164.5 46.8 %collective-permute-start.22 = (bf16[4,2,512,128]{3,2,1,0:T(8,128)(2,1)}, bf16[4,2,512,128]{3,2,1,0:T(8,128)(2,1)S(1)}, u32[]{:S(2)}, u32[]{:S(2)}) collective-permute-start(bf16[4,2,512,128]{3,2,1,0:T(8,128)(2,1)} %get-tuple-element.261.refs_1_), channel_id=1, source_target_pairs={{0,4},{1,5},{2,6},{3,7},{4,0},{5,1},{6,2},{7,3},{8,12},{9,13},{10,... | collective-permute-start | bytes 3145736 | tf_op jit(solution)/shard_map/ppermute | solution.py:344
  183.7 27.5 %copy-start.3 = (bf16[4,2,512,128]{3,2,1,0:T(8,128)(2,1)S(1)}, bf16[4,2,512,128]{3,2,1,0:T(8,128)(2,1)}, u32[]{:S(2)}) copy-start(bf16[4,2,512,128]{3,2,1,0:T(8,128)(2,1)} %get-tuple-element.271.refs_1_) | copy-start | bytes 3145732
  199.0 236.0 %collective-permute-start.20 = (bf16[4,2,512,128]{3,2,1,0:T(8,128)(2,1)}, bf16[4,2,512,128]{3,2,1,0:T(8,128)(2,1)S(1)}, u32[]{:S(2)}, u32[]{:S(2)}) collective-permute-start(bf16[4,2,512,128]{3,2,1,0:T(8,128)(2,1)} %get-tuple-element.251.refs_3_), channel_id=1, source_target_pairs={{0,8},{8,0},{16,24},{24,16},{1,9},{9,1},{17,25},{25,17},{2,10},{10... | collective-permute-start | bytes 3145736 | tf_op jit(solution)/shard_map/ppermute | solution.py:344
  199.6 235.4 %collective-permute-start.21 = (bf16[4,2,512,128]{3,2,1,0:T(8,128)(2,1)}, bf16[4,2,512,128]{3,2,1,0:T(8,128)(2,1)S(1)}, u32[]{:S(2)}, u32[]{:S(2)}) collective-permute-start(bf16[4,2,512,128]{3,2,1,0:T(8,128)(2,1)} %get-tuple-element.251.refs_3_), channel_id=1, source_target_pairs={{0,16},{8,24},{16,0},{24,8},{1,17},{9,25},{17,1},{25,9},{2,18},{10... | collective-permute-start | bytes 3145736 | tf_op jit(solution)/shard_map/ppermute | solution.py:344
  211.3 218.8 %copy-start.1 = (bf16[4,2,512,128]{3,2,1,0:T(8,128)(2,1)}, bf16[4,2,512,128]{3,2,1,0:T(8,128)(2,1)S(1)}, u32[]{:S(2)}) copy-start(bf16[4,2,512,128]{3,2,1,0:T(8,128)(2,1)S(1)} %collective-permute-done.22.refs_0_.refs_4_) | copy-start | bytes 3145732
  211.3 681.0 %collective-permute-start.23 = (bf16[4,2,512,128]{3,2,1,0:T(8,128)(2,1)S(1)}, bf16[4,2,512,128]{3,2,1,0:T(8,128)(2,1)S(1)}, u32[]{:S(2)}, u32[]{:S(2)}) collective-permute-start(bf16[4,2,512,128]{3,2,1,0:T(8,128)(2,1)S(1)} %copy-done.3), channel_id=1, source_target_pairs={{0,4},{1,5},{2,6},{3,7},{4,0},{5,1},{6,2},{7,3},{8,12},{9,13},{10,... | collective-permute-start | bytes 3145736 | tf_op jit(solution)/shard_map/ppermute | solution.py:344
  430.1 463.4 %collective-permute-start.27 = (bf16[512,128]{1,0:T(8,128)(2,1)}, bf16[512,128]{1,0:T(8,128)(2,1)S(1)}, u32[]{:S(2)}, u32[]{:S(2)}) collective-permute-start(bf16[512,128]{1,0:T(8,128)(2,1)} %get-tuple-element.279), channel_id=1, source_target_pairs={{0,1},{1,0},{2,3},{3,2},{4,5},{5,4},{6,7},{7,6},{8,9},{9,8},{10,11... | collective-permute-start | bytes 393224 | tf_op jit(solution)/shard_map/ppermute | solution.py:344
  432.5 461.7 %collective-permute-start.28 = (bf16[512,128]{1,0:T(8,128)(2,1)}, bf16[512,128]{1,0:T(8,128)(2,1)S(1)}, u32[]{:S(2)}, u32[]{:S(2)}) collective-permute-start(bf16[512,128]{1,0:T(8,128)(2,1)} %get-tuple-element.280), channel_id=1, source_target_pairs={{0,2},{1,3},{2,0},{3,1},{4,6},{5,7},{6,4},{7,5},{8,10},{9,11},{10,... | collective-permute-start | bytes 393224 | tf_op jit(solution)/shard_map/ppermute | solution.py:344
  434.9 459.4 %collective-permute-start.29 = (bf16[512,128]{1,0:T(8,128)(2,1)}, bf16[512,128]{1,0:T(8,128)(2,1)S(1)}, u32[]{:S(2)}, u32[]{:S(2)}) collective-permute-start(bf16[512,128]{1,0:T(8,128)(2,1)} %get-tuple-element.281), channel_id=1, source_target_pairs={{0,3},{1,2},{2,1},{3,0},{4,7},{5,6},{6,5},{7,4},{8,11},{9,10},{10,... | collective-permute-start | bytes 393224 | tf_op jit(solution)/shard_map/ppermute | solution.py:344
  673.4 222.3 %collective-permute-start.33 = (bf16[512,128]{1,0:T(8,128)(2,1)}, bf16[512,128]{1,0:T(8,128)(2,1)S(1)}, u32[]{:S(2)}, u32[]{:S(2)}) collective-permute-start(bf16[512,128]{1,0:T(8,128)(2,1)} %get-tuple-element.285), channel_id=1, source_target_pairs={{0,1},{1,0},{2,3},{3,2},{4,5},{5,4},{6,7},{7,6},{8,9},{9,8},{10,11... | collective-permute-start | bytes 393224 | tf_op jit(solution)/shard_map/ppermute | solution.py:344
  673.8 218.5 %copy-start.40 = (bf16[512,128]{1,0:T(8,128)(2,1)S(1)}, bf16[512,128]{1,0:T(8,128)(2,1)}, u32[]{:S(2)}) copy-start(bf16[512,128]{1,0:T(8,128)(2,1)} %get-tuple-element.286) | copy-start | bytes 393220
  673.8 219.7 %copy-start.39 = (bf16[512,128]{1,0:T(8,128)(2,1)S(1)}, bf16[512,128]{1,0:T(8,128)(2,1)}, u32[]{:S(2)}) copy-start(bf16[512,128]{1,0:T(8,128)(2,1)} %get-tuple-element.287) | copy-start | bytes 393220
  892.3 222.6 %collective-permute-start.34 = (bf16[512,128]{1,0:T(8,128)(2,1)S(1)}, bf16[512,128]{1,0:T(8,128)(2,1)S(1)}, u32[]{:S(2)}, u32[]{:S(2)}) collective-permute-start(bf16[512,128]{1,0:T(8,128)(2,1)S(1)} %copy-done.40), channel_id=1, source_target_pairs={{0,2},{1,3},{2,0},{3,1},{4,6},{5,7},{6,4},{7,5},{8,10},{9,11},{10,... | collective-permute-start | bytes 393224 | tf_op jit(solution)/shard_map/ppermute | solution.py:344
  893.5 221.3 %copy-start.11 = (bf16[512,128]{1,0:T(8,128)(2,1)}, bf16[512,128]{1,0:T(8,128)(2,1)S(1)}, u32[]{:S(2)}) copy-start(bf16[512,128]{1,0:T(8,128)(2,1)S(1)} %collective-permute-done.27.refs_1_) | copy-start | bytes 393220
  893.5 221.5 %collective-permute-start.35 = (bf16[512,128]{1,0:T(8,128)(2,1)S(1)}, bf16[512,128]{1,0:T(8,128)(2,1)S(1)}, u32[]{:S(2)}, u32[]{:S(2)}) collective-permute-start(bf16[512,128]{1,0:T(8,128)(2,1)S(1)} %copy-done.39), channel_id=1, source_target_pairs={{0,3},{1,2},{2,1},{3,0},{4,7},{5,6},{6,5},{7,4},{8,11},{9,10},{10,... | collective-permute-start | bytes 393224 | tf_op jit(solution)/shard_map/ppermute | solution.py:344
  894.2 220.6 %copy-start.12 = (bf16[512,128]{1,0:T(8,128)(2,1)}, bf16[512,128]{1,0:T(8,128)(2,1)S(1)}, u32[]{:S(2)}) copy-start(bf16[512,128]{1,0:T(8,128)(2,1)S(1)} %collective-permute-done.28.refs_2_) | copy-start | bytes 393220
  894.2 222.2 %collective-permute-start.30 = (bf16[512,128]{1,0:T(8,128)(2,1)}, bf16[512,128]{1,0:T(8,128)(2,1)S(1)}, u32[]{:S(2)}, u32[]{:S(2)}) collective-permute-start(bf16[512,128]{1,0:T(8,128)(2,1)} %get-tuple-element.282), channel_id=1, source_target_pairs={{0,1},{1,0},{2,3},{3,2},{4,5},{5,4},{6,7},{7,6},{8,9},{9,8},{10,11... | collective-permute-start | bytes 393224 | tf_op jit(solution)/shard_map/ppermute | solution.py:344
  894.3 220.5 %copy-start.13 = (bf16[512,128]{1,0:T(8,128)(2,1)}, bf16[512,128]{1,0:T(8,128)(2,1)S(1)}, u32[]{:S(2)}) copy-start(bf16[512,128]{1,0:T(8,128)(2,1)S(1)} %collective-permute-done.29.refs_3_) | copy-start | bytes 393220
  894.3 222.8 %collective-permute-start.31 = (bf16[512,128]{1,0:T(8,128)(2,1)}, bf16[512,128]{1,0:T(8,128)(2,1)S(1)}, u32[]{:S(2)}, u32[]{:S(2)}) collective-permute-start(bf16[512,128]{1,0:T(8,128)(2,1)} %get-tuple-element.283), channel_id=1, source_target_pairs={{0,2},{1,3},{2,0},{3,1},{4,6},{5,7},{6,4},{7,5},{8,10},{9,11},{10,... | collective-permute-start | bytes 393224 | tf_op jit(solution)/shard_map/ppermute | solution.py:344
  895.7 219.2 %copy-start.14 = (bf16[512,128]{1,0:T(8,128)(2,1)}, bf16[512,128]{1,0:T(8,128)(2,1)S(1)}, u32[]{:S(2)}) copy-start(bf16[512,128]{1,0:T(8,128)(2,1)S(1)} %collective-permute-done.33.refs_9_) | copy-start | bytes 393220
  895.7 221.4 %collective-permute-start.32 = (bf16[512,128]{1,0:T(8,128)(2,1)}, bf16[512,128]{1,0:T(8,128)(2,1)S(1)}, u32[]{:S(2)}, u32[]{:S(2)}) collective-permute-start(bf16[512,128]{1,0:T(8,128)(2,1)} %get-tuple-element.284), channel_id=1, source_target_pairs={{0,3},{1,2},{2,1},{3,0},{4,7},{5,6},{6,5},{7,4},{8,11},{9,10},{10,... | collective-permute-start | bytes 393224 | tf_op jit(solution)/shard_map/ppermute | solution.py:344
  1114.9 5.5 collective-permute-start.24
  1115.0 5.4 collective-permute-start.25
  1116.4 6.9 collective-permute-start.26
  (29 other events, 224.5 us)
